TPU v7x, 32 devices: a whole 2x2x4 slice. The times are simulated.
32 devices in a mesh: batch: 8 (over z, y), wide: 4 (over x, core).
Axes of the slice: x: 2, y: 2, z: 4, core: 2. Of those that a mesh axis runs over, the one named last changes fastest.
Arguments:
- layer_in: bfloat16 [32768, 512], P(('batch', 'wide')), may hold values from -6 to 6
- dual_in: float32 [32768, 512], P(('batch', 'wide')), may hold values from -6 to 6
- long_count: int32 [32], P(('batch', 'wide')), may hold values from 0 to 1, as said below
- w_query: bfloat16 [512, 512], replicated, may hold values from -0.375 to 0.375
- w_key: bfloat16 [512, 512], replicated, may hold values from -0.375 to 0.375
- w_value: bfloat16 [512, 512], replicated, may hold values from -0.25 to 0.25
- w_output: bfloat16 [512, 512], replicated, may hold values from -0.75 to 0.75
- gain_one: float32 [512], replicated, may hold values from 0.5 to 1.5
- shift_one: float32 [512], replicated, may hold values from -3 to 3
- w_in: bfloat16 [512, 2048], P(None, 'wide'), may hold values from -0.25 to 0.25
- bias_in: bfloat16 [2048], P('wide'), may hold values from -3 to 3
- w_out: bfloat16 [2048, 512], P('wide'), may hold values from -0.1875 to 0.1875
- bias_out: float32 [512], replicated, may hold values from -3 to 3
- gain_two: float32 [512], replicated, may hold values from 0.5 to 1.5
- shift_two: float32 [512], replicated, may hold values from -3 to 3
- cot_main: float32 [32768, 512], P(('batch', 'wide')), may hold values from -6 to 6
- cot_dual: float32 [32768, 512], P(('batch', 'wide')), may hold values from -6 to 6
Outputs:
- layer_out: bfloat16 [32768, 512], P(('batch', 'wide'))
- dual_out: float32 [32768, 512], P(('batch', 'wide'))
- grad_layer_in: float32 [32768, 512], P(('batch', 'wide'))
- grad_w_query: float32 [512, 512], replicated
- grad_w_key: float32 [512, 512], replicated
- grad_w_value: float32 [512, 512], replicated
- grad_w_output: float32 [512, 512], replicated
- grad_gain_one: float32 [512], replicated
- grad_shift_one: float32 [512], replicated
- grad_w_in: float32 [512, 2048], P(None, 'wide')
- grad_bias_in: float32 [2048], P('wide')
- grad_w_out: float32 [2048, 512], P('wide')
- grad_bias_out: float32 [512], replicated
- grad_gain_two: float32 [512], replicated
- grad_shift_two: float32 [512], replicated
Inputs may be any that keep to these rules, and one draw needn't show every extreme that they name: `long_count`: each entry counts the 1024-token sequences that open a device's 1024 tokens; the rest of those tokens are 256-token sequences.
All inputs are finite; a program needn't handle non-finite values.
Results may differ from a plain program's by a relative error of at most 0.017.
The roundings to bfloat16 on the way count: a program that leaves them out, or rounds other values in their place, can miss the bound.
Values may be sent and summed in bfloat16 or wider, within the bound.
A program may use at most 256 MiB of HBM per device.

v0:
```python
import jax
import jax.numpy as jnp
from jax import lax
from jax.sharding import PartitionSpec as P

HEADS = 8
HEAD_DIM = 64
LONG = 1024
SHORT = 256


EPSILON = 1e-05
MASKED = -1000000000.0


def plain_dot(left, right):
    return jnp.dot(left, right, preferred_element_type=jnp.float32)


def over_rows(left, right):
    return lax.dot_general(
        left, right, (((0,), (0,)), ((), ())), preferred_element_type=jnp.float32
    )


def against(left, right):
    return lax.dot_general(
        left, right, (((1,), (1,)), ((), ())), preferred_element_type=jnp.float32
    )


def smooth_unit(value):
    return 0.5 * value * (1.0 + jax.scipy.special.erf(value * 0.7071067811865476))


def smooth_slope(value):
    return (
        0.5 * (1.0 + jax.scipy.special.erf(value * 0.7071067811865476))
        + value * jnp.exp(-0.5 * value * value) * 0.3989422804014327
    )


def visible_mask(count, windows):
    positions = jnp.arange(LONG, dtype=jnp.int32)
    is_long = jnp.arange(windows, dtype=jnp.int32) < count
    segment = jnp.where(is_long[:, None], jnp.int32(0), positions[None, :] // SHORT)
    causal = positions[:, None] >= positions[None, :]
    same_seq = segment[:, :, None] == segment[:, None, :]
    return (causal[None] & same_seq)[:, None]


def norm_forward(hidden, gain, shift):
    centre = hidden - jnp.mean(hidden, axis=-1, keepdims=True)
    spread = jnp.mean(centre * centre, axis=-1, keepdims=True)
    inverse = lax.rsqrt(spread + EPSILON)
    normed = centre * inverse
    return (normed * gain + shift, normed, inverse)


def norm_backward(grad, normed, inverse, gain):
    scaled = grad * gain
    inner = (
        scaled
        - jnp.mean(scaled, axis=-1, keepdims=True)
        - normed * jnp.mean(scaled * normed, axis=-1, keepdims=True)
    )
    return (inner * inverse, jnp.sum(grad * normed, axis=0), jnp.sum(grad, axis=0))


def masked_scores(query, keyed, visible, factor):
    scores = (
        jnp.einsum("wqhd,wkhd->whqk", query, keyed, preferred_element_type=jnp.float32) * factor
    )
    return jnp.where(visible, scores, MASKED)


def body(
    layer_in,
    dual_in,
    long_count,
    w_query,
    w_key,
    w_value,
    w_output,
    gain_one,
    shift_one,
    w_in,
    bias_in,
    w_out,
    bias_out,
    gain_two,
    shift_two,
    cot_main,
    cot_dual,
):
    tokens = layer_in.shape[0]
    width = layer_in.shape[1]
    windows = tokens // LONG
    shape_four = (windows, LONG, HEADS, HEAD_DIM)
    factor = jnp.float32(HEAD_DIM) ** (-0.5)
    visible = visible_mask(long_count[0], windows)
    inputs = layer_in.astype(jnp.float32)
    query = plain_dot(layer_in, w_query).astype(jnp.bfloat16).reshape(shape_four)
    keyed = plain_dot(layer_in, w_key).astype(jnp.bfloat16).reshape(shape_four)
    values = plain_dot(layer_in, w_value).astype(jnp.bfloat16).reshape(shape_four)
    scores = masked_scores(query, keyed, visible, factor)
    peak = jnp.max(scores, axis=-1, keepdims=True)
    expo = jnp.exp(scores - peak)
    total = jnp.sum(expo, axis=-1, keepdims=True)
    log_total = peak + jnp.log(total)
    probs_low = (expo / total).astype(jnp.bfloat16)
    mixed = jnp.einsum("whqk,wkhd->wqhd", probs_low, values, preferred_element_type=jnp.float32)
    mixed = mixed.reshape(tokens, width).astype(jnp.bfloat16)
    attended = plain_dot(mixed, w_output)
    first, normed_one, inverse_one = norm_forward(inputs + attended, gain_one, shift_one)
    dual_mid = dual_in + attended
    first_low = first.astype(jnp.bfloat16)
    w_in_all, bias_in_all, w_out_all = (
        lax.all_gather(w_in, "wide", axis=1, tiled=True),
        lax.all_gather(bias_in, "wide", axis=0, tiled=True),
        lax.all_gather(w_out, "wide", axis=0, tiled=True),
    )
    pre = plain_dot(first_low, w_in_all) + bias_in_all.astype(jnp.float32)
    active_low = smooth_unit(pre).astype(jnp.bfloat16)
    branch = plain_dot(active_low, w_out_all) + bias_out
    second, normed_two, inverse_two = norm_forward(first + branch, gain_two, shift_two)
    layer_out = second.astype(jnp.bfloat16)
    dual_out = dual_mid + branch
    g_sum, grad_gain_two, grad_shift_two = norm_backward(
        cot_main, normed_two, inverse_two, gain_two
    )
    g_branch = (g_sum + cot_dual).astype(jnp.bfloat16)
    grad_bias_out = jnp.sum(g_branch.astype(jnp.float32), axis=0)
    g_pre = (against(g_branch, w_out_all) * smooth_slope(pre)).astype(jnp.bfloat16)
    grad_w_out_all = over_rows(active_low, g_branch)
    grad_w_in_all = over_rows(first_low, g_pre)
    grad_bias_in_all = jnp.sum(g_pre.astype(jnp.float32), axis=0)
    g_ffn = against(g_pre, w_in_all)
    grad_w_in, grad_bias_in, grad_w_out = (
        lax.psum_scatter(
            grad_w_in_all.astype(jnp.bfloat16), "wide", scatter_dimension=1, tiled=True
        ).astype(jnp.float32),
        lax.psum_scatter(
            grad_bias_in_all.astype(jnp.bfloat16), "wide", scatter_dimension=0, tiled=True
        ).astype(jnp.float32),
        lax.psum_scatter(
            grad_w_out_all.astype(jnp.bfloat16), "wide", scatter_dimension=0, tiled=True
        ).astype(jnp.float32),
    )
    grad_w_in, grad_bias_in, grad_w_out = (
        lax.psum(grad_w_in.astype(jnp.bfloat16), "batch").astype(jnp.float32),
        lax.psum(grad_bias_in.astype(jnp.bfloat16), "batch").astype(jnp.float32),
        lax.psum(grad_w_out.astype(jnp.bfloat16), "batch").astype(jnp.float32),
    )
    g_first = g_sum + g_ffn
    g_resid, grad_gain_one, grad_shift_one = norm_backward(
        g_first, normed_one, inverse_one, gain_one
    )
    g_attended = (g_resid + cot_dual).astype(jnp.bfloat16)
    grad_w_output = over_rows(mixed, g_attended)
    g_mixed = against(g_attended, w_output).astype(jnp.bfloat16).reshape(shape_four)
    scores = masked_scores(query, keyed, visible, factor)
    probs = jnp.exp(scores - log_total)
    g_probs = jnp.einsum("wqhd,wkhd->whqk", g_mixed, values, preferred_element_type=jnp.float32)
    g_values = jnp.einsum(
        "whqk,wqhd->wkhd", probs.astype(jnp.bfloat16), g_mixed, preferred_element_type=jnp.float32
    )
    g_values = g_values.astype(jnp.bfloat16).reshape(tokens, width)
    centred = jnp.sum(g_probs * probs, axis=-1, keepdims=True)
    g_scores = (probs * (g_probs - centred)).astype(jnp.bfloat16)
    g_query = (
        jnp.einsum("whqk,wkhd->wqhd", g_scores, keyed, preferred_element_type=jnp.float32) * factor
    )
    g_query = g_query.astype(jnp.bfloat16).reshape(tokens, width)
    g_keyed = (
        jnp.einsum("whqk,wqhd->wkhd", g_scores, query, preferred_element_type=jnp.float32) * factor
    )
    g_keyed = g_keyed.astype(jnp.bfloat16).reshape(tokens, width)
    grad_w_query = over_rows(layer_in, g_query)
    grad_w_key = over_rows(layer_in, g_keyed)
    grad_w_value = over_rows(layer_in, g_values)
    grad_layer_in = (
        g_resid + against(g_query, w_query) + against(g_keyed, w_key) + against(g_values, w_value)
    )
    summed = lax.psum(
        (
            grad_w_query,
            grad_w_key,
            grad_w_value,
            grad_w_output,
            grad_gain_one,
            grad_shift_one,
            grad_bias_out,
            grad_gain_two,
            grad_shift_two,
        ),
        ("batch", "wide"),
    )
    return (
        layer_out,
        dual_out,
        grad_layer_in,
        summed[0],
        summed[1],
        summed[2],
        summed[3],
        summed[4],
        summed[5],
        grad_w_in,
        grad_bias_in,
        grad_w_out,
        summed[6],
        summed[7],
        summed[8],
    )


def solution(mesh):
    return jax.shard_map(
        body,
        mesh=mesh,
        in_specs=(
            P(("batch", "wide"), None),
            P(("batch", "wide"), None),
            P(("batch", "wide")),
            P(),
            P(),
            P(),
            P(),
            P(),
            P(),
            P(None, "wide"),
            P("wide"),
            P("wide", None),
            P(),
            P(),
            P(),
            P(("batch", "wide"), None),
            P(("batch", "wide"), None),
        ),
        out_specs=(
            P(("batch", "wide"), None),
            P(("batch", "wide"), None),
            P(("batch", "wide"), None),
            P(),
            P(),
            P(),
            P(),
            P(),
            P(),
            P(None, "wide"),
            P("wide"),
            P("wide", None),
            P(),
            P(),
            P(),
        ),
        check_vma=False,
    )
```

profile of v0, /device:TPU:1, one launch (start us, length us, event | category | flops | bytes accessed | tf_op | source)
XLA Modules:
  0.0 456.8 jit_solution(14855953730202328719)
XLA Ops:
  14.2 14.2 %fusion.27 = (f32[8,1024]{1,0:T(8,128)S(1)}, f32[8,1024,1024]{1,2,0:T(8,128)}) fusion(bf16[1024,8,64]{0,2,1:T(8,128)(2,1)S(1)} %bitcast.79, bf16[1024,8,64]{0,2,1:T(8,128)(2,1)S(1)} %bitcast.77, pred[1024,1024]{0,1:T(8,128)(4,1)S(1)} %fusion.12), kind=kOutput, calls=%fused_computation.78 | convolution fusion | flops 1098899456 | bytes 36732928 | tf_op jit(solution)/shard_map/wqhd,wkhd->whqk/dot_general | solution.py:72
  28.4 13.1 %fusion = f32[8,1024]{1,0:T(8,128)S(1)} fusion(f32[8,1024,1024]{1,2,0:T(8,128)} %get-tuple-element.72, f32[8,1024]{1,0:T(8,128)S(1)} %get-tuple-element.71), kind=kLoop, calls=%fused_computation.6 | loop fusion | flops 16769024 | bytes 33619968 | tf_op jit(solution)/shard_map/reduce_sum | solution.py:109
  41.5 15.3 %fusion.17 = bf16[8,64,1024]{2,1,0:T(8,128)(2,1)} fusion(bf16[1024,8,64]{0,2,1:T(8,128)(2,1)S(1)} %bitcast.89, f32[8,1024,1024]{1,2,0:T(8,128)} %get-tuple-element.72, f32[8,1024]{1,0:T(8,128)S(1)} %fusion, f32[8,1024]{1,0:T(8,128)S(1)} %get-tuple-element.71), kind=kOutput, calls=%fused_computation.54 | convolution fusion | flops 1099431936 | bytes 35717120 | tf_op jit(solution)/shard_map/whqk,wkhd->wqhd/dot_general | solution.py:112
  56.8 2.4 copy.52
  59.3 5.9 %all-gather = bf16[4,1,512]{2,1,0:T(2,128)(2,1)S(1)} all-gather(bf16[1,1,512]{2,1,0:T(2,128)(2,1)S(1)} %reshape.302), channel_id=1, replica_groups=mesh['batch'=8,'wide'=4] {'wide'}, dimensions={0}, use_global_device_ids=true | all-gather | bytes 5120 | tf_op jit(solution)/shard_map/all_gather | solution.py:120
  67.0 3.0 copy.56
  71.9 3.6 fusion.26
  76.2 7.7 %multiply_convert_fusion.1 = (bf16[1024,2048]{1,0:T(8,128)(2,1)}, f32[1024,2048]{1,0:T(8,128)}) fusion(f32[2048]{0:T(1024)S(1)} %bitcast.93, bf16[512,2048]{1,0:T(8,128)(2,1)} %all-gather.4.cloned.1.call-done, f32[1024,512]{0,1:T(8,128)S(1)} %get-tuple-element.68, f32[512]{0:T(512)S(1)} %copy-done.36, f32[512]{0:T(512)S(1)} %copy-done.31, ...), kind=kOutput, calls=%fused_computation.18 | convolution fusion | flops 2162688000 | bytes 16797696 | tf_op jit(solution)/shard_map/dot_general | solution.py:17
  83.9 8.1 %fusion.25 = (f32[1024]{0:T(1024)S(1)}, f32[1024,512]{0,1:T(8,128)S(1)}, f32[1024,512]{0,1:T(8,128)}) fusion(f32[512]{0:T(512)S(1)} %copy-done.35, f32[512]{0:T(512)S(1)} %copy-done.36, f32[512]{0:T(512)S(1)} %copy-done.31, f32[1024]{0:T(1024)S(1)} %add_rsqrt_fusion.1, f32[1024,512]{0,1:T(8,128)S(1)} %get-tuple-element.68, ...), kind=kOutput, calls=%fused_computation.76 | convolution fusion | flops 2152201216 | bytes 16795648 | tf_op jit(solution)/shard_map/dot_general | solution.py:17
  99.0 3.8 convolution_convert_fusion
  103.4 8.1 %fusion.28 = (bf16[2048]{0:T(1024)(128)(2,1)S(1)}, bf16[1024,2048]{1,0:T(8,128)(2,1)S(1)}) fusion(f32[1024,2048]{1,0:T(8,128)} %get-tuple-element.75, f32[2048]{0:T(1024)S(1)} %bitcast.94, bf16[1024,512]{0,1:T(8,128)(2,1)} %copy-done.17, bf16[2048,512]{1,0:T(8,128)(2,1)} %all-gather.6.cloned.1.call-done), kind=kOutput, calls=%fused_computation.79 | convolution fusion | flops 2172647424 | bytes 15740928 | tf_op jit(solution)/shard_map/dot_general | solution.py:27
  111.5 3.5 multiply_reduce_fusion.2
  119.8 3.8 convolution_convert_fusion.1
  123.6 22.7 %multiply_reduce_fusion = (f32[8,1024]{1,0:T(8,128)S(1)}, f32[8,1024,1024]{1,2,0:T(8,128)}) fusion(f32[8,1024,1024]{1,2,0:T(8,128)} %get-tuple-element.72, f32[8,1024]{1,0:T(8,128)S(1)} %log_add_fusion, bf16[1024,8,64]{0,2,1:T(8,128)(2,1)} %bitcast.81, bf16[1024,8,64]{0,2,1:T(8,128)(2,1)} %bitcast.90), kind=kOutput, calls=%fused_computation.1 | convolution fusion | flops 1098899456 | bytes 69271552 | tf_op jit(solution)/shard_map/wqhd,wkhd->whqk/dot_general | solution.py:164
  146.4 29.0 %multiply_convert_fusion = bf16[8,1024,1024]{1,2,0:T(8,128)(2,1)} fusion(f32[8,1024,1024]{1,2,0:T(8,128)} %get-tuple-element.78, f32[8,1024,1024]{1,2,0:T(8,128)} %get-tuple-element.72, f32[8,1024]{1,0:T(8,128)S(1)} %get-tuple-element.77, f32[8,1024]{1,0:T(8,128)S(1)} %log_add_fusion), kind=kLoop, calls=%fused_computation | loop fusion | flops 33554432 | bytes 83951616 | tf_op jit(solution)/shard_map/convert_element_type | solution.py:170
  175.4 14.7 %fusion.14 = bf16[8,64,1024]{2,1,0:T(8,128)(2,1)} fusion(bf16[1024,8,64]{0,2,1:T(8,128)(2,1)} %bitcast.82, f32[8,1024,1024]{1,2,0:T(8,128)} %get-tuple-element.72, f32[8,1024]{1,0:T(8,128)S(1)} %log_add_fusion), kind=kOutput, calls=%fused_computation.49 | convolution fusion | flops 1091043328 | bytes 35684352 | tf_op jit(solution)/shard_map/whqk,wqhd->wkhd/dot_general | solution.py:165
  190.1 3.2 convolution_bitcast_fusion
  193.3 12.3 %multiply_convert_fusion.2 = bf16[8,64,1024]{2,1,0:T(8,128)(2,1)} fusion(bf16[1024,8,64]{0,2,1:T(8,128)(2,1)} %bitcast.80, bf16[8,1024,1024]{1,2,0:T(8,128)(2,1)} %multiply_convert_fusion), kind=kOutput, calls=%fused_computation.28 | convolution fusion | flops 1074790400 | bytes 18874368 | tf_op jit(solution)/shard_map/whqk,wqhd->wkhd/dot_general | solution.py:176
  205.6 3.3 convolution_bitcast_fusion.1
  208.9 8.9 %multiply_convert_fusion.3 = bf16[8,64,1024]{2,1,0:T(8,128)(2,1)S(1)} fusion(bf16[1024,8,64]{0,2,1:T(8,128)(2,1)S(1)} %bitcast.78, bf16[8,1024,1024]{1,2,0:T(8,128)(2,1)} %multiply_convert_fusion), kind=kOutput, calls=%fused_computation.29 | convolution fusion | flops 1074790400 | bytes 18874368 | tf_op jit(solution)/shard_map/whqk,wkhd->wqhd/dot_general | solution.py:172
  223.8 3.3 fusion.31
  227.0 3.3 copy.67
  230.3 5.8 %all-reduce = bf16[2048]{0:T(1024)(128)(2,1)S(1)} all-reduce(bf16[2048]{0:T(1024)(128)(2,1)S(1)} %get-tuple-element.79), channel_id=3, replica_groups=mesh['batch'=8,'wide'=4] {'wide'}, use_global_device_ids=true, to_apply=%region_22.23.clone | all-reduce | flops 2048 | bytes 8192
  236.2 18.2 %psum.91 = bf16[512]{0:T(512)(128)(2,1)S(1)} all-reduce(bf16[512]{0:T(512)(128)(2,1)S(1)} %dynamic-slice.1), channel_id=1, replica_groups=mesh['batch'=8,'wide'=4] {'batch'}, use_global_device_ids=true, to_apply=%region_23.24 | all-reduce | flops 512 | bytes 2048 | tf_op jit(solution)/shard_map/psum | solution.py:152
  255.0 2.3 copy.66
  259.6 4.1 add_add_fusion
  263.8 2.9 copy.68
  266.6 42.4 %all-reduce.1 = (f32[512]{0:T(512)}, f32[512]{0:T(512)}, f32[512]{0:T(512)}, f32[512]{0:T(512)}, f32[512]{0:T(512)}) all-reduce(f32[512]{0:T(512)S(1)} %get-tuple-element.47, f32[512]{0:T(512)S(1)} %get-tuple-element.51, f32[512]{0:T(512)S(1)} %get-tuple-element.63, ...), channel_id=1, replica_groups=mesh['batch'=8,'wide'=4] {'batch','wide'}, use_global_device_ids=true, to_apply=%region_16.17 | all-reduce | flops 2560 | bytes 20480 | tf_op jit(solution)/shard_map/psum | solution.py:185
  309.0 54.0 %all-reduce.7.cloned.1.call-done = (f32[512,512]{0,1:T(8,128)}, f32[512,512]{0,1:T(8,128)}, f32[512,512]{0,1:T(8,128)}, f32[512,512]{1,0:T(8,128)}) async-done(((f32[512,512]{0,1:T(8,128)}, f32[512,512]{0,1:T(8,128)}, f32[512,512]{0,1:T(8,128)}, f32[512,512]{1,0:T(8,128)}), (f32[512,512]{0,1:T(8,128)}, f32[512,512]{0,1:T(8,128)}, f32[512,512]{0,1:T(8,128)}, ...) | async-done | bytes 4194320 | tf_op jit(solution)/shard_map/psum | solution.py:185
  363.1 2.7 copy.69
  368.4 76.1 %all-reduce.9.cloned.1.call-done = (bf16[512,512]{1,0:T(8,128)(2,1)}, bf16[512,512]{1,0:T(8,128)(2,1)}) async-done(((bf16[512,512]{1,0:T(8,128)(2,1)}, bf16[512,512]{1,0:T(8,128)(2,1)}), (bf16[512,512]{1,0:T(8,128)(2,1)}, bf16[512,512]{1,0:T(8,128)(2,1)})) %all-reduce.9.cloned.1.call-update) | async-done | bytes 1048592 | tf_op jit(solution)/shard_map/psum | solution.py:151
  446.6 2.1 convert_element_type.145
  (128 shorter events, 36.6 us)
Async XLA Ops:
  7.2 64.7 %copy-start = (bf16[512,512]{1,0:T(8,128)(2,1)S(1)}, bf16[512,512]{1,0:T(8,128)(2,1)}, u32[]{:S(2)}) copy-start(bf16[512,512]{1,0:T(8,128)(2,1)} %param.23) | copy-start | bytes 1572868
  7.2 2.9 copy-start.18
  7.2 68.7 %all-gather.4.cloned.1.call-start = ((), (), s32[]{:S(2)}) async-start(), calls=%async_computation.2 | async-start | bytes 2621440 | tf_op jit(solution)/shard_map/all_gather | solution.py:119
  7.9 76.0 %all-gather.6.cloned.1.call-start = ((), (), s32[]{:S(2)}) async-start(), calls=%async_computation.3 | async-start | bytes 2621440 | tf_op jit(solution)/shard_map/all_gather | solution.py:121
  8.7 3.3 copy-start.25
  8.7 215.0 %reduce-scatter.5.cloned.1.call-start = ((), (), s32[]{:S(2)}) async-start(), calls=%async_computation.5 | async-start | bytes 2621440 | tf_op jit(solution)/shard_map/reduce_scatter | solution.py:146
  8.7 3.2 copy-start.19
  13.4 15.0 %copy-start.10 = (bf16[1024,512]{0,1:T(8,128)(2,1)}, bf16[1024,512]{0,1:T(8,128)(2,1)S(1)}, u32[]{:S(2)}) copy-start(bf16[1024,512]{0,1:T(8,128)(2,1)S(1)} %convolution_convert_fusion.3) | copy-start | bytes 3145732
  14.2 27.4 %copy-start.16 = (bf16[1024,512]{0,1:T(8,128)(2,1)}, bf16[1024,512]{0,1:T(8,128)(2,1)S(1)}, u32[]{:S(2)}) copy-start(bf16[1024,512]{0,1:T(8,128)(2,1)S(1)} %convolution_convert_fusion.5) | copy-start | bytes 3145732
  41.5 17.7 %copy-start.33 = (bf16[512]{0:T(512)(128)(2,1)S(1)}, bf16[512]{0:T(512)(128)(2,1)}, u32[]{:S(2)}) copy-start(bf16[512]{0:T(512)(128)(2,1)} %param.27) | copy-start | bytes 3076
  56.8 8.4 %copy-start.8 = (f32[1024,512]{1,0:T(8,128)S(1)}, f32[1024,512]{1,0:T(8,128)}, u32[]{:S(2)}) copy-start(f32[1024,512]{1,0:T(8,128)} %param.32) | copy-start | bytes 6291460
  67.0 3.0 copy-start.15
  76.2 7.7 %copy-start.35 = (f32[512]{0:T(512)S(1)}, f32[512]{0:T(512)}, u32[]{:S(2)}) copy-start(f32[512]{0:T(512)} %param.29) | copy-start | bytes 6148
  92.1 3.2 copy-start.3
  92.1 2.3 copy-start.1
  92.1 2.3 copy-start.30
  96.0 3.0 copy-start.38
  102.8 120.9 %reduce-scatter.3.cloned.1.call-start = ((), (), s32[]{:S(2)}) async-start(), calls=%async_computation.4 | async-start | bytes 2621440 | tf_op jit(solution)/shard_map/reduce_scatter | solution.py:140
  103.4 8.1 %copy-start.2 = (f32[1024,512]{0,1:T(8,128)S(1)}, f32[1024,512]{0,1:T(8,128)}, u32[]{:S(2)}) copy-start(f32[1024,512]{0,1:T(8,128)} %copy.55) | copy-start | bytes 6291460
  103.4 8.1 %copy-start.4 = (f32[1024,512]{0,1:T(8,128)S(1)}, f32[1024,512]{0,1:T(8,128)}, u32[]{:S(2)}) copy-start(f32[1024,512]{0,1:T(8,128)} %copy-done.3) | copy-start | bytes 6291460
  103.4 8.1 %copy-start.34 = (bf16[512,2048]{1,0:T(8,128)(2,1)S(1)}, bf16[512,2048]{1,0:T(8,128)(2,1)}, u32[]{:S(2)}) copy-start(bf16[512,2048]{1,0:T(8,128)(2,1)} %all-gather.4.cloned.1.call-done) | copy-start | bytes 6291460
  111.5 3.5 copy-start.6
  123.6 239.4 %all-reduce.7.cloned.1.call-start = ((), (), s32[]{:S(2)}) async-start(), calls=%async_computation.6 | async-start | bytes 8388608 | tf_op jit(solution)/shard_map/psum | solution.py:185
  205.6 3.3 copy-start.11
  208.9 9.9 %copy-start.20 = (bf16[1024,512]{1,0:T(8,128)(2,1)S(1)}, bf16[1024,512]{1,0:T(8,128)(2,1)}, u32[]{:S(2)}) copy-start(bf16[1024,512]{1,0:T(8,128)(2,1)} %param.17) | copy-start | bytes 3145732
  220.5 3.2 copy-start.26
  220.5 223.9 %all-reduce.9.cloned.1.call-start = ((), (), s32[]{:S(2)}) async-start(), calls=%async_computation.7 | async-start | bytes 2097152 | tf_op jit(solution)/shard_map/psum | solution.py:151
  230.3 27.0 %copy-start.27 = (bf16[512,512]{1,0:T(8,128)(2,1)S(1)}, bf16[512,512]{1,0:T(8,128)(2,1)}, u32[]{:S(2)}) copy-start(bf16[512,512]{1,0:T(8,128)(2,1)} %param.20) | copy-start | bytes 1572868
  257.3 2.3 copy-start.29
  363.0 2.7 copy-start.23
  363.0 4.0 copy-start.22
  368.4 80.4 %copy-start.21 = (f32[512,512]{1,0:T(8,128)S(1)}, f32[512,512]{1,0:T(8,128)}, u32[]{:S(2)}) copy-start(f32[512,512]{1,0:T(8,128)} %get-tuple-element.89) | copy-start | bytes 3145732
  (13 other events, 19.4 us)
Sparse Core Ops, SparseCore 0:
  9.6 25.0 all-gather.3
  36.3 22.5 all-gather.5
  103.0 32.5 reduce-scatter.4
  138.7 31.3 reduce-scatter.2
  220.6 142.3 all-reduce.6
  366.5 77.9 all-reduce.8
where the time goes:
time: 466 us; the launch traced here: 457 us
  matrix products  151 us (32%)
  waiting for transfers between devices  132 us (28%)
  blocking collectives  72.3 us (16%)
  other arithmetic  53.5 us (11%)
  local copies, waits for them, and re-layouts  31.3 us (7%)
  between operations  16.2 us (3%)
    psum x1, waiting for transfers between devices, body(): lax.psum(grad_w_in.astype(jnp.bfloat16), 'batch').astype(jnp.float32)  76.1 us
    psum x1, waiting for transfers between devices, body(): lax.psum((grad_w_query, grad_w_key, grad_w_value, grad_w_output, grad_gai...  54 us
    psum x1, blocking collectives, body(): lax.psum((grad_w_query, grad_w_key, grad_w_value, grad_w_output, grad_gai...  42.4 us
    unnamed x92, local copies, waits for them, and re-layouts  31.3 us
    convert_element_type x1, other arithmetic, body(): g_scores = (probs * (g_probs - centred)).astype(jnp.bfloat16)  29 us
    dot_general x6, matrix products, plain_dot(): return jnp.dot(left, right, preferred_element_type=jnp.float32)  22.8 us
    dot_general x6, matrix products, against(): lax.dot_general(left, right, (((1,), (1,)), ((), ())), preferred_element_...  22.7 us
    dot_general x1, matrix products, body(): jnp.einsum('wqhd,wkhd->whqk', g_mixed, values, preferred_element_type=jnp...  22.7 us
  transfers between devices with their start and end apart: 6, of which 2 were waited for; matrix products, arithmetic and copies ran while one was open for 46% of the time, Pallas kernels for 0%

commit v1 on v0

v1 whole, which is shorter than its diff:
```python
import functools

import jax
import jax.numpy as jnp
from jax import lax
from jax.experimental import pallas as pl
from jax.experimental.pallas import tpu as pltpu
from jax.sharding import PartitionSpec as P

HEADS = 8
HEAD_DIM = 64
LONG = 1024
SHORT = 256
EPSILON = 1e-05
MASKED = -1000000000.0
BLOCK = 256
GROUP = 4

bf16 = jnp.bfloat16
f32 = jnp.float32


def contract(left, right, a, b):
    return lax.dot_general(
        left, right, (((a,), (b,)), ((), ())), preferred_element_type=f32
    )


def dot_nn(left, right):
    return contract(left, right, 1, 0)


def dot_nt(left, right):
    return contract(left, right, 1, 1)


def dot_tn(left, right):
    return contract(left, right, 0, 0)


def dot_tt(left, right):
    return contract(left, right, 0, 1)


def rows_of(block):
    return slice(block * BLOCK, (block + 1) * BLOCK)


def head_of(head):
    return pl.ds(pl.multiple_of(head * HEAD_DIM, HEAD_DIM), HEAD_DIM)


def block_rows(block):
    return pl.ds(pl.multiple_of(block * BLOCK, BLOCK), BLOCK)


def each(count, step):
    lax.fori_loop(0, count, lambda at, _: (step(at), 0)[1], 0)


def row_mean(value):
    return jnp.mean(value, axis=-1, keepdims=True)


def col_sum(value):
    return jnp.sum(value, axis=0, keepdims=True)


class Net:
    def start(self):
        pass

    def weights(self, block):
        pass

    def ffn_grad(self, which, block):
        pass

    def attn_grad(self, chunk):
        pass

    def tick(self, place):
        pass

    def finish(self):
        pass


def layer(r, net, order):
    tokens, width = r.x.shape
    blocks = tokens // BLOCK
    hidden = len(order)

    def project(block):
        cols = rows_of(block)
        xb = r.x[cols]
        r.qt[:, cols] = (dot_tt(r.wq[...], xb) * HEAD_DIM**-0.5).astype(bf16)
        r.kt[:, cols] = dot_tt(r.wk[...], xb).astype(bf16)
        r.vt[:, cols] = dot_tt(r.wv[...], xb).astype(bf16)

    r.wait("x", "wq", "wk", "wv")
    for block in range(blocks):
        project(block)
        net.tick(("project", block))

    row_at = lax.broadcasted_iota(jnp.int32, (BLOCK, BLOCK), 0)
    col_at = lax.broadcasted_iota(jnp.int32, (BLOCK, BLOCK), 1)
    causal = row_at <= col_at
    away = jnp.where(r.count > 0, 0.0, 2e9).astype(f32)

    def soften(head, qb):
        hs = head_of(head)
        query = r.qt[hs, rows_of(qb)]
        parts = []
        peak_off = None
        for tb in range(qb + 1):
            scores = dot_tn(r.kt[hs, rows_of(tb)], query)
            if tb == qb:
                scores = jnp.where(causal, scores, MASKED)
            parts.append(scores)
            peak = jnp.max(scores, axis=0, keepdims=True)
            if tb < qb:
                peak_off = peak if peak_off is None else jnp.maximum(peak_off, peak)
        if peak_off is not None:
            peak = jnp.maximum(peak, peak_off - away)
        total = jnp.zeros((1, BLOCK), f32)
        for tb in range(qb + 1):
            expo = jnp.exp(parts[tb] - (peak if tb == qb else peak + away))
            total += jnp.sum(expo, axis=0, keepdims=True)
            r.p[qb][head, rows_of(tb)] = expo.astype(bf16)
        r.inv_total[pl.ds(head, 1), rows_of(qb)] = 1.0 / total

    def mix(head, qb):
        hs = head_of(head)
        mixed = dot_nn(r.vt[hs, : (qb + 1) * BLOCK], r.p[qb][head])
        mixed *= r.inv_total[pl.ds(head, 1), rows_of(qb)]
        r.mt[hs, rows_of(qb)] = mixed.astype(bf16)

    def attend(group):
        for at in range(GROUP + 1):
            head = group * GROUP + at
            for qb in range(blocks):
                if at < GROUP:
                    soften(head, qb)
                if at > 0:
                    mix(head - 1, qb)

    each(HEADS // GROUP, attend)

    r.wait("wo", "dual")
    gain_one, shift_one = r.vec[0:1], r.vec[1:2]
    def norm_block(block):
        rows = block_rows(block)
        attended = dot_tn(r.mt[:, rows], r.wo[...])
        r.dual[rows] += attended
        hidden_one = r.x[rows].astype(f32) + attended
        centre = hidden_one - row_mean(hidden_one)
        inverse = lax.rsqrt(row_mean(centre * centre) + EPSILON)
        normed = centre * inverse
        r.n1[rows] = normed
        r.i1[rows] = inverse
        r.fl[rows] = (normed * gain_one + shift_one).astype(bf16)

    each(blocks, norm_block)

    for step, j in enumerate(order):
        net.weights(step)

        def half_block(block, j=j):
            rows = block_rows(block)
            pre = dot_nn(r.fl[rows], r.wi[j]) + r.bi[j]
            phi = 0.5 + 0.5 * lax.erf(pre * 0.7071067811865476)
            bell = jnp.exp(-0.5 * pre * pre) * 0.3989422804014327
            r.act[j, rows] = (pre * phi).astype(bf16)
            r.slope[j, rows] = (phi + pre * bell).astype(bf16)

        each(blocks, half_block)

    r.wait("cm", "cd")
    gain_two, shift_two, bias_out = r.vec[3:4], r.vec[4:5], r.vec[2:3]
    r.gvec[...] = jnp.zeros_like(r.gvec)

    def second_block(block):
        rows = block_rows(block)
        branch = dot_nn(r.act[order[0], rows], r.wo2[order[0]])
        for j in order[1:]:
            branch += dot_nn(r.act[j, rows], r.wo2[j])
        branch += bias_out
        r.dual[rows] += branch
        hidden_two = r.n1[rows] * gain_one + shift_one + branch
        centre = hidden_two - row_mean(hidden_two)
        inverse = lax.rsqrt(row_mean(centre * centre) + EPSILON)
        normed = centre * inverse
        r.lo[rows] = (normed * gain_two + shift_two).astype(bf16)
        grad = r.cm[rows]
        r.gvec[3:4] += col_sum(grad * normed)
        r.gvec[4:5] += col_sum(grad)
        scaled = grad * gain_two
        g_sum = inverse * (
            scaled - row_mean(scaled) - normed * row_mean(scaled * normed)
        )
        r.cm[rows] = g_sum
        g_branch = (g_sum + r.cd[rows]).astype(bf16)
        r.gb[rows] = g_branch
        r.gvec[2:3] += col_sum(g_branch.astype(f32))

    each(blocks, second_block)
    r.put("lo")
    r.put("dual")

    for step, j in enumerate(order):
        r.gwo2[j] = dot_tn(r.act[j], r.gb[...]).astype(bf16)
        net.ffn_grad(0, step)
    for step, j in enumerate(order):
        r.gbi[j] = jnp.zeros_like(r.gbi[j])

        def pre_block(block, j=j):
            rows = block_rows(block)
            g_act = dot_nt(r.gb[rows], r.wo2[j])
            g_pre = (g_act * r.slope[j, rows].astype(f32)).astype(bf16)
            r.slope[j, rows] = g_pre
            r.gbi[j] += col_sum(g_pre.astype(f32))

        each(blocks, pre_block)
        r.gwi[j] = dot_tn(r.fl[...], r.slope[j]).astype(bf16)
        net.ffn_grad(1, step)

    def first_block(block):
        rows = block_rows(block)
        g_first = dot_nt(r.slope[order[0], rows], r.wi[order[0]])
        for j in order[1:]:
            g_first += dot_nt(r.slope[j, rows], r.wi[j])
        g_first += r.cm[rows]
        normed = r.n1[rows]
        r.gvec[0:1] += col_sum(g_first * normed)
        r.gvec[1:2] += col_sum(g_first)
        scaled = g_first * gain_one
        g_resid = r.i1[rows] * (
            scaled - row_mean(scaled) - normed * row_mean(scaled * normed)
        )
        r.cm[rows] = g_resid
        g_att = (g_resid + r.cd[rows]).astype(bf16)
        r.gatt[rows] = g_att
        g_mixed = dot_nt(r.wo[...], g_att)
        g_mixed = g_mixed.reshape(HEADS, HEAD_DIM, BLOCK) * r.inv_total[:, rows][:, None]
        g_mixed = g_mixed.reshape(width, BLOCK).astype(bf16)
        r.got[:, rows] = g_mixed
        centred = g_mixed.astype(f32) * r.mt[:, rows].astype(f32)
        r.centred[:, rows] = jnp.sum(centred.reshape(HEADS, HEAD_DIM, BLOCK), axis=1)

    each(blocks, first_block)
    r.gw_o[...] = dot_nn(r.mt[...], r.gatt[...]).astype(bf16)
    net.attn_grad(0)
    r.xt[...] = r.x[...].T

    def back_values(head, tb):
        hs = head_of(head)
        total = None
        for qb in range(tb, blocks):
            part = dot_nt(r.got[hs, rows_of(qb)], r.p[qb][head, rows_of(tb)])
            total = part if total is None else total + part
        r.dvt[hs, rows_of(tb)] = total.astype(bf16)

    def back_scores(head, qb, slot):
        hs = head_of(head)
        got = r.got[hs, rows_of(qb)]
        centred = r.centred[pl.ds(head, 1), rows_of(qb)]
        for tb in range(qb + 1):
            g_probs = dot_tn(r.vt[hs, rows_of(tb)], got)
            probs = r.p[qb][head, rows_of(tb)].astype(f32)
            slot[qb][rows_of(tb)] = (probs * (g_probs - centred)).astype(bf16)

    def back_query(head, qb, slot):
        hs = head_of(head)
        g_query = dot_nn(r.kt[hs, : (qb + 1) * BLOCK], slot[qb][...])
        r.dqt[hs, rows_of(qb)] = (g_query * HEAD_DIM**-0.5).astype(bf16)

    def back_keys(head, tb, slot):
        hs = head_of(head)
        total = None
        for qb in range(tb, blocks):
            part = dot_nt(r.qt[hs, rows_of(qb)], slot[qb][rows_of(tb)])
            total = part if total is None else total + part
        r.dkt[hs, rows_of(tb)] = total.astype(bf16)

    half = width // 2

    def value_heads(group):
        for at in range(GROUP):
            for tb in range(blocks):
                back_values(group * GROUP + at, tb)

    each(HEADS // GROUP, value_heads)
    r.gw_v[...] = dot_nt(r.xt[...], r.dvt[...]).astype(bf16)
    net.attn_grad(1)

    def score_heads(group):
        for at in range(GROUP + 1):
            head = group * GROUP + at
            for block in range(blocks):
                if at < GROUP:
                    back_scores(head, block, r.gs[at % 2])
                if at > 0:
                    back_query(head - 1, block, r.gs[(at - 1) % 2])
                    back_keys(head - 1, block, r.gs[(at - 1) % 2])
        rows = pl.ds(pl.multiple_of(group * half, half), half)
        r.gw_qk[group, :, :half] = dot_nt(r.xt[...], r.dqt[rows]).astype(bf16)
        r.gw_qk[group, :, half:] = dot_nt(r.xt[...], r.dkt[rows]).astype(bf16)

    each(HEADS // GROUP, score_heads)

    def input_block(block):
        rows = block_rows(block)
        grad = dot_tt(r.dqt[:, rows], r.wq[...])
        grad += dot_tt(r.dkt[:, rows], r.wk[...])
        grad += dot_tt(r.dvt[:, rows], r.wv[...])
        r.cm[rows] += grad

    each(blocks, input_block)
    r.put("cm")
    net.finish()
    r.drain()


class Refs:
    def __init__(self, names, refs):
        self.__dict__.update(zip(names, refs))
        self.pending = {}
        self.out = []

    def fetch(self, name, source, target, sem):
        copy = pltpu.make_async_copy(source, target, sem)
        copy.start()
        self.pending[name] = copy

    def wait(self, *names):
        for name in names:
            if name in self.pending:
                self.pending.pop(name).wait()

    def put(self, name):
        source, target, sem = self.outs[name]
        copy = pltpu.make_async_copy(source, target, sem)
        copy.start()
        self.out.append(copy)

    def drain(self):
        for copy in self.out:
            copy.wait()


FETCHED = ("x", "wq", "wk", "wv", "wo", "wi", "wo2", "dual", "cm", "cd")


def scratch_list(tokens, width, hidden, piece):
    vmem = pltpu.VMEM
    blocks = tokens // BLOCK
    names = {
        "x": vmem((tokens, width), bf16),
        "wq": vmem((width, width), bf16),
        "wk": vmem((width, width), bf16),
        "wv": vmem((width, width), bf16),
        "wo": vmem((width, width), bf16),
        "wi": vmem((hidden, width, piece), bf16),
        "wo2": vmem((hidden, piece, width), bf16),
        "dual": vmem((tokens, width), f32),
        "cm": vmem((tokens, width), f32),
        "cd": vmem((tokens, width), f32),
        "qt": vmem((width, tokens), bf16),
        "kt": vmem((width, tokens), bf16),
        "vt": vmem((width, tokens), bf16),
        "mt": vmem((width, tokens), bf16),
        "inv_total": vmem((HEADS, tokens), f32),
        "centred": vmem((HEADS, tokens), f32),
        "n1": vmem((tokens, width), f32),
        "i1": vmem((tokens, 1), f32),
        "fl": vmem((tokens, width), bf16),
        "act": vmem((hidden, tokens, piece), bf16),
        "slope": vmem((hidden, tokens, piece), bf16),
        "gb": vmem((tokens, width), bf16),
        "lo": vmem((tokens, width), bf16),
        "gatt": vmem((tokens, width), bf16),
        "got": vmem((width, tokens), bf16),
        "dqt": vmem((width, tokens), bf16),
        "dkt": vmem((width, tokens), bf16),
        "dvt": vmem((width, tokens), bf16),
        "xt": vmem((width, tokens), bf16),
    }
    for qb in range(blocks):
        names[f"p{qb}"] = vmem((HEADS, (qb + 1) * BLOCK, BLOCK), bf16)
        names[f"g{qb}"] = vmem(((qb + 1) * BLOCK, BLOCK), bf16)
        names[f"h{qb}"] = vmem(((qb + 1) * BLOCK, BLOCK), bf16)
    return names


def plain_kernel(names, blocks, order, *refs):
    r = Refs(names, refs)
    r.count = r.count_ref[0]
    sems = r.sems
    for at, name in enumerate(FETCHED):
        r.fetch(name, getattr(r, name + "_hbm"), getattr(r, name), sems.at[at])
    r.p = [getattr(r, f"p{qb}") for qb in range(blocks)]
    r.gs = [[getattr(r, f"{s}{qb}") for qb in range(blocks)] for s in "gh"]
    base = len(FETCHED)
    r.outs = {
        "lo": (r.lo, r.lo_hbm, sems.at[base]),
        "dual": (r.dual, r.dual_out, sems.at[base + 1]),
        "cm": (r.cm, r.gx_out, sems.at[base + 2]),
    }
    r.wait("wi", "wo2")
    layer(r, Net(), order)


def plain_layer(x, dual, count, wq, wk, wv, wo, vec, wi, bi, wo2, cm, cd):
    tokens, width = x.shape
    hidden, _, piece = wi.shape
    blocks = tokens // BLOCK
    anyspace = pl.BlockSpec(memory_space=pl.ANY)
    vm = pl.BlockSpec(memory_space=pltpu.VMEM)
    sm = pl.BlockSpec(memory_space=pltpu.SMEM)
    ins = {
        "x_hbm": (x, anyspace),
        "wq_hbm": (wq, anyspace),
        "wk_hbm": (wk, anyspace),
        "wv_hbm": (wv, anyspace),
        "wo_hbm": (wo, anyspace),
        "wi_hbm": (wi, anyspace),
        "wo2_hbm": (wo2, anyspace),
        "dual_hbm": (dual, anyspace),
        "cm_hbm": (cm, anyspace),
        "cd_hbm": (cd, anyspace),
        "count_ref": (count, sm),
        "vec": (vec, vm),
        "bi": (bi, vm),
    }
    shape = jax.ShapeDtypeStruct
    outs = {
        "lo_hbm": (shape((tokens, width), bf16), anyspace),
        "dual_out": (shape((tokens, width), f32), anyspace),
        "gx_out": (shape((tokens, width), f32), anyspace),
        "gw_o": (shape((width, width), bf16), vm),
        "gw_v": (shape((width, width), bf16), vm),
        "gw_qk": (shape((2, width, width), bf16), vm),
        "gwi": (shape((hidden, width, piece), bf16), vm),
        "gwo2": (shape((hidden, piece, width), bf16), vm),
        "gvec": (shape((8, width), f32), vm),
        "gbi": (shape((hidden, 1, piece), f32), vm),
    }
    scratch = scratch_list(tokens, width, hidden, piece)
    scratch["sems"] = pltpu.SemaphoreType.DMA((len(FETCHED) + 3,))
    names = list(ins) + list(outs) + list(scratch)
    return pl.pallas_call(
        functools.partial(plain_kernel, names, blocks, tuple(range(hidden))),
        out_shape=[o[0] for o in outs.values()],
        in_specs=[i[1] for i in ins.values()],
        out_specs=[o[1] for o in outs.values()],
        scratch_shapes=list(scratch.values()),
        compiler_params=pltpu.CompilerParams(vmem_limit_bytes=63 << 20),
        cost_estimate=pl.CostEstimate(flops=25 * 10**9, bytes_accessed=30 << 20, transcendentals=12 << 20),
    )(*[i[0] for i in ins.values()])


def unpack(summed_qk, half):
    gq = jnp.concatenate([summed_qk[0][:, :half], summed_qk[1][:, :half]], axis=1)
    gk = jnp.concatenate([summed_qk[0][:, half:], summed_qk[1][:, half:]], axis=1)
    return gq, gk


def plain_body(layer_in, dual_in, long_count, w_query, w_key, w_value, w_output, gain_one, shift_one,
               w_in, bias_in, w_out, bias_out, gain_two, shift_two, cot_main, cot_dual):
    width = layer_in.shape[1]
    piece = width
    w_in_all = lax.all_gather(w_in, "wide", axis=1, tiled=True)
    bias_all = lax.all_gather(bias_in, "wide", axis=0, tiled=True)
    w_out_all = lax.all_gather(w_out, "wide", axis=0, tiled=True)
    hidden = w_in_all.shape[1] // piece
    wi = w_in_all.reshape(width, hidden, piece).transpose(1, 0, 2)
    wo2 = w_out_all.reshape(hidden, piece, width)
    bi = bias_all.astype(f32).reshape(hidden, 1, piece)
    zero = jnp.zeros_like(gain_one)
    vec = jnp.stack([gain_one, shift_one, bias_out, gain_two, shift_two, zero, zero, zero])
    lo, dual, gx, gw_o, gw_v, gw_qk, gwi, gwo2, gvec, gbi = plain_layer(
        layer_in, dual_in, long_count, w_query, w_key, w_value, w_output, vec, wi, bi, wo2, cot_main, cot_dual)
    gwi = gwi.transpose(1, 0, 2).reshape(w_in_all.shape)
    gwo2 = gwo2.reshape(w_out_all.shape)
    gwi = lax.psum(lax.psum_scatter(gwi, "wide", scatter_dimension=1, tiled=True), "batch").astype(f32)
    gwo2 = lax.psum(lax.psum_scatter(gwo2, "wide", scatter_dimension=0, tiled=True), "batch").astype(f32)
    gbi = lax.psum(lax.psum_scatter(gbi.reshape(-1), "wide", scatter_dimension=0, tiled=True), "batch")
    gw_o, gw_v, gw_qk, gvec = lax.psum((gw_o, gw_v, gw_qk, gvec), ("batch", "wide"))
    gq, gk = unpack(gw_qk.astype(f32), width // 2)
    return (lo, dual, gx, gq, gk, gw_v.astype(f32), gw_o.astype(f32), gvec[0], gvec[1], gwi, gbi, gwo2, gvec[2], gvec[3], gvec[4])


def solution(mesh):
    tokens = P(("batch", "wide"), None)
    return jax.shard_map(
        plain_body,
        mesh=mesh,
        in_specs=(tokens, tokens, P(("batch", "wide")), P(), P(), P(), P(), P(), P(), P(None, "wide"), P("wide"),
                  P("wide", None), P(), P(), P(), tokens, tokens),
        out_specs=(tokens, tokens, tokens, P(), P(), P(), P(), P(), P(), P(None, "wide"), P("wide"),
                   P("wide", None), P(), P(), P()),
        check_vma=False,
    )
```

time: 466 us -> 428 us (0.918); the launches traced: 457 us -> 426 us
  matrix products: 151 us -> 0 us
  waiting for transfers between devices: 132 us -> 252 us
  Pallas kernels: 0 us -> 63.4 us
  other arithmetic: 53.5 us -> 8.74 us
  local copies, waits for them, and re-layouts: 31.3 us -> 14.9 us
    dot_general x24 -> x0, matrix products: 151 us -> none  [the longest x6 22.8 us: plain_dot(): return jnp.dot(left, right, preferred_element_type=jnp.float32)]
    psum x2, waiting for transfers between devices: 130 us -> 213 us  [the longest x1 138 us: plain_body(): lax.psum((gw_o, gw_v, gw_qk, gvec), ('batch', 'wide'))]
    pallas_call x0 -> x1, Pallas kernels: none -> 63.4 us  [plain_layer(): pl.pallas_call(functools.partial(plain_kernel, names, blocks, tuple(range...]
    all_gather x2, waiting for transfers between devices: 0.02 us -> 37.2 us  [the longest x1 20 us: plain_body(): w_out_all = lax.all_gather(w_out, 'wide', axis=0, tiled=True)]
    convert_element_type x6 -> x4, other arithmetic: 34.5 us -> 5.94 us  [the longest x1 2.14 us: plain_body(): lax.psum(lax.psum_scatter(gwo2, 'wide', scatter_dimension=0, tiled=True),...]
    unnamed x92 -> x27, local copies, waits for them, and re-layouts: 31.3 us -> 4.99 us
    reduce_sum x6 -> x0, other arithmetic: 18.3 us -> none  [the longest x1 13.1 us: body(): total = jnp.sum(expo, axis=-1, keepdims=True)]
  transfers between devices with their start and end apart: 6 -> 6, of which waited for: 2 -> 4; matrix products, arithmetic and copies ran while one was open for 46% -> 3% of each run, Pallas kernels for 0% -> 0%
where the time goes in v1:
time: 428 us; the launch traced here: 426 us
  waiting for transfers between devices  252 us (59%)
  blocking collectives  70.4 us (16%)
  Pallas kernels  63.4 us (15%)
  between operations  15.7 us (4%)
  local copies, waits for them, and re-layouts  14.9 us (3%)
  other arithmetic  8.74 us (2%)
    psum x1, waiting for transfers between devices, plain_body(): lax.psum((gw_o, gw_v, gw_qk, gvec), ('batch', 'wide'))  138 us
    psum x1, waiting for transfers between devices, plain_body(): lax.psum(lax.psum_scatter(gwi, 'wide', scatter_dimension=1, tiled=True),...  75.3 us
    pallas_call x1, Pallas kernels, plain_layer(): pl.pallas_call(functools.partial(plain_kernel, names, blocks, tuple(range...  63.4 us
    psum x1, blocking collectives, plain_body(): lax.psum((gw_o, gw_v, gw_qk, gvec), ('batch', 'wide'))  40.9 us
    all_gather x1, waiting for transfers between devices, plain_body(): w_out_all = lax.all_gather(w_out, 'wide', axis=0, tiled=True)  20 us
    psum x1, blocking collectives, plain_body(): lax.psum(lax.psum_scatter(gbi.reshape(-1), 'wide', scatter_dimension=0, t...  18.2 us
    all_gather x1, waiting for transfers between devices, plain_body(): w_in_all = lax.all_gather(w_in, 'wide', axis=1, tiled=True)  17.2 us
  transfers between devices with their start and end apart: 6, of which 4 were waited for; matrix products, arithmetic and copies ran while one was open for 3% of the time, Pallas kernels for 0%

profile of v1, /device:TPU:1, one launch (start us, length us, event | category | flops | bytes accessed | tf_op | source)
XLA Modules:
  0.0 425.8 jit_solution(17386713014103853327)
XLA Ops:
  7.3 2.0 copy.36
  9.4 0.0 all-gather.6.cloned.1.call-start
  9.4 0.7 all-gather.6.cloned.1.call-update
  10.1 0.0 reduce-scatter.3.cloned.1.call-start
  10.2 6.0 %all-gather = bf16[4,1,512]{2,1,0:T(2,128)(2,1)S(1)} all-gather(bf16[1,1,512]{2,1,0:T(2,128)(2,1)S(1)} %reshape.59), channel_id=1, replica_groups=mesh['batch'=8,'wide'=4] {'wide'}, dimensions={0}, use_global_device_ids=true | all-gather | bytes 5120 | tf_op jit(solution)/shard_map/all_gather | solution.py:474
  16.1 0.6 reshape.61.refs_12_
  17.5 0.6 stack.27.refs_11_
  18.1 17.2 %all-gather.4.cloned.1.call-done = bf16[512,2048]{0,1:T(8,128)(2,1)} async-done(((bf16[512,512]{0,1:T(8,128)(2,1)}), bf16[512,2048]{0,1:T(8,128)(2,1)}) %all-gather.4.cloned.1.call-update) | async-done | bytes 2097168 | tf_op jit(solution)/shard_map/all_gather | solution.py:473
  35.3 4.2 copy.37
  39.5 20.0 %all-gather.6.cloned.1.call-done = bf16[2048,512]{1,0:T(8,128)(2,1)} async-done(((bf16[512,512]{1,0:T(8,128)(2,1)}), bf16[2048,512]{1,0:T(8,128)(2,1)}) %all-gather.6.cloned.1.call-update) | async-done | bytes 2097168 | tf_op jit(solution)/shard_map/all_gather | solution.py:475
  59.5 63.4 %shard_map.280 = (bf16[1024,512]{1,0:T(8,128)(2,1)}, f32[1024,512]{1,0:T(8,128)}, f32[1024,512]{1,0:T(8,128)}, bf16[512,512]{1,0:T(8,128)(2,1)}, bf16[512,512]{1...) custom-call(bf16[1024,512]{1,0:T(8,128)(2,1)} %refs_0_.1, ...), custom_call_target="tpu_custom_call" | custom-call | flops 24999999488 | bytes 31457280 | tf_op jit(solution)/shard_map/pallas_call | solution.py:452
  123.0 4.2 copy.38
  127.2 0.0 reduce-scatter.5.cloned.1.call-start
  127.2 0.5 reduce-scatter.5.cloned.1.call-update
  127.8 0.5 all-reduce.6.cloned.1.call-update
  128.4 0.6 dynamic-slice
  129.6 5.4 %all-reduce = f32[2048]{0:T(1024)S(1)} all-reduce(f32[2048]{0:T(1024)S(1)} %bitcast.27), channel_id=3, replica_groups=mesh['batch'=8,'wide'=4] {'wide'}, use_global_device_ids=true, to_apply=%region_6.0.clone | all-reduce | flops 2048 | bytes 16384
  135.0 0.1 dynamic-slice.1
  135.1 18.2 %psum.54 = f32[512]{0:T(512)} all-reduce(f32[512]{0:T(512)S(1)} %dynamic-slice.1), channel_id=1, replica_groups=mesh['batch'=8,'wide'=4] {'batch'}, use_global_device_ids=true, to_apply=%region_7.0 | all-reduce | flops 512 | bytes 4096 | tf_op jit(solution)/shard_map/psum | solution.py:488
  153.2 40.9 %psum.52 = f32[8,512]{1,0:T(8,128)S(1)} all-reduce(f32[8,512]{1,0:T(8,128)S(1)} %copy-done.2), channel_id=1, replica_groups=mesh['batch'=8,'wide'=4] {'batch','wide'}, use_global_device_ids=true, to_apply=%region_3.0 | all-reduce | flops 4096 | bytes 32768 | tf_op jit(solution)/shard_map/psum | solution.py:489
  194.2 0.6 fusion.2
  194.8 138.1 %all-reduce.6.cloned.1.call-done = (bf16[2,512,512]{2,1,0:T(8,128)(2,1)}, bf16[512,512]{1,0:T(8,128)(2,1)}, bf16[512,512]{1,0:T(8,128)(2,1)}) async-done(((bf16[2,512,512]{2,1,0:T(8,128)(2,1)}, bf16[512,512]{1,0:T(8,128)(2,1)}, bf16[512,512]{1,0:T(8,128)(2,1)}), (bf16[2,512,512]{2,1,0:T(8,128)(2,1)}, bf16[512,512]{1,0:T(8,128)(2,1)}, bf16[512,512]{1,0:T(8,128)(2,1)})) %all-reduce.6.cloned.1.call-update) | async-done | bytes 2097168 | tf_op jit(solution)/shard_map/psum | solution.py:489
  333.0 1.6 convert_element_type.16
  334.6 1.1 convert_element_type.17
  335.7 1.1 convert_element_type.18
  336.8 0.2 slice_bitcast_fusion.1
  337.0 0.2 fusion
  337.2 1.1 pad_maximum_fusion.1
  338.2 1.1 pad_maximum_fusion
  339.3 75.3 %all-reduce.8.cloned.1.call-done = (bf16[512,512]{0,1:T(8,128)(2,1)}, bf16[512,512]{1,0:T(8,128)(2,1)}) async-done(((bf16[512,512]{0,1:T(8,128)(2,1)}, bf16[512,512]{1,0:T(8,128)(2,1)}), (bf16[512,512]{0,1:T(8,128)(2,1)}, bf16[512,512]{1,0:T(8,128)(2,1)})) %all-reduce.8.cloned.1.call-update) | async-done | bytes 1048592 | tf_op jit(solution)/shard_map/psum | solution.py:486
  414.6 2.1 convert_element_type.20
  416.7 2.2 copy.39
  (33 shorter events, 0.3 us)
Async XLA Ops:
  7.2 3.0 copy-start.9
  7.2 10.2 %copy-start.4 = (f32[512]{0:T(512)S(1)}, f32[512]{0:T(512)}, u32[]{:S(2)}) copy-start(f32[512]{0:T(512)} %param.24) | copy-start | bytes 6148
  7.2 10.2 %copy-start.5 = (f32[512]{0:T(512)S(1)}, f32[512]{0:T(512)}, u32[]{:S(2)}) copy-start(f32[512]{0:T(512)} %param.25) | copy-start | bytes 6148
  7.2 10.2 %copy-start.6 = (f32[512]{0:T(512)S(1)}, f32[512]{0:T(512)}, u32[]{:S(2)}) copy-start(f32[512]{0:T(512)} %param.29) | copy-start | bytes 6148
  7.2 10.2 %copy-start.7 = (f32[512]{0:T(512)S(1)}, f32[512]{0:T(512)}, u32[]{:S(2)}) copy-start(f32[512]{0:T(512)} %param.30) | copy-start | bytes 6148
  7.2 10.2 %copy-start.8 = (f32[512]{0:T(512)S(1)}, f32[512]{0:T(512)}, u32[]{:S(2)}) copy-start(f32[512]{0:T(512)} %param.31) | copy-start | bytes 6148
  7.2 28.1 %all-gather.4.cloned.1.call-start = ((), (), s32[]{:S(2)}) async-start(), calls=%async_computation.2 | async-start | bytes 2621440 | tf_op jit(solution)/shard_map/all_gather | solution.py:473
  9.4 50.1 %all-gather.6.cloned.1.call-start = ((), (), s32[]{:S(2)}) async-start(), calls=%async_computation.3 | async-start | bytes 2621440 | tf_op jit(solution)/shard_map/all_gather | solution.py:475
  10.1 184.0 %reduce-scatter.3.cloned.1.call-start = ((), (), s32[]{:S(2)}) async-start(), calls=%async_computation.4 | async-start | bytes 2621440 | tf_op jit(solution)/shard_map/reduce_scatter | solution.py:486
  127.2 67.0 %reduce-scatter.5.cloned.1.call-start = ((), (), s32[]{:S(2)}) async-start(), calls=%async_computation.5 | async-start | bytes 2621440 | tf_op jit(solution)/shard_map/reduce_scatter | solution.py:487
  127.2 1.2 copy-start.10
  127.2 2.4 copy-start.3
  127.2 26.0 %copy-start.2 = (f32[8,512]{1,0:T(8,128)S(1)}, f32[8,512]{1,0:T(8,128)}, u32[]{:S(2)}) copy-start(f32[8,512]{1,0:T(8,128)} %get-tuple-element.31) | copy-start | bytes 49156
  127.7 205.2 %all-reduce.6.cloned.1.call-start = ((), (), s32[]{:S(2)}) async-start(), calls=%async_computation.6 | async-start | bytes 4194304 | tf_op jit(solution)/shard_map/psum | solution.py:489
  128.3 286.3 %all-reduce.8.cloned.1.call-start = ((), (), s32[]{:S(2)}) async-start(), calls=%async_computation.7 | async-start | bytes 2097152 | tf_op jit(solution)/shard_map/psum | solution.py:486
  333.0 1.6 copy-start.1
  333.0 2.7 copy-start
Sparse Core Ops, SparseCore 0:
  10.2 25.0 all-gather.3
  36.9 22.5 all-gather.5
  127.3 31.0 reduce-scatter.2
  160.9 31.5 reduce-scatter.4
  199.2 133.6 all-reduce.5
  336.8 77.7 all-reduce.7

commit v2 on v1

v2 whole, which is shorter than its diff:
```python
import functools

import jax
import jax.numpy as jnp
from jax import lax
from jax.experimental import pallas as pl
from jax.experimental.pallas import tpu as pltpu
from jax.sharding import PartitionSpec as P

HEADS = 8
HEAD_DIM = 64
EPSILON = 1e-05
MASKED = -1000000000.0
BLOCK = 256
HALF = 512
PARTS = 4
PRE_UNROLL = 1
HALF_UNROLL = NORM_UNROLL = SECOND_UNROLL = FIRST_UNROLL = INPUT_UNROLL = 2
Y_FIRST = (True, True, True, False, False, False)

bf16 = jnp.bfloat16
f32 = jnp.float32


def contract(left, right, a, b):
    return lax.dot_general(
        left, right, (((a,), (b,)), ((), ())), preferred_element_type=f32
    )


def dot_nn(left, right):
    return contract(left, right, 1, 0)


def dot_nt(left, right):
    return contract(left, right, 1, 1)


def dot_tn(left, right):
    return contract(left, right, 0, 0)


def dot_tt(left, right):
    return contract(left, right, 0, 1)


def span_of(at, size):
    if isinstance(at, int):
        return slice(at * size, (at + 1) * size)
    return pl.ds(pl.multiple_of(at * size, size), size)


def rows_of(block):
    return span_of(block, BLOCK)


def head_of(head):
    return span_of(head, HEAD_DIM)


def split(block):
    return block // 2, span_of(block % 2, BLOCK)


def each(count, step, unroll=1):
    def several(at, _):
        for k in range(unroll):
            step(at * unroll + k)
        return 0

    lax.fori_loop(0, count // unroll, several, 0)


def row_mean(value):
    return jnp.mean(value, axis=-1, keepdims=True)


def col_sum(value):
    return jnp.sum(value, axis=0, keepdims=True)


def joined(value):
    return value.reshape(value.shape[0] * value.shape[1], value.shape[2])


def layer(r, net):
    tokens, width = r.x.shape
    blocks = tokens // BLOCK
    hidden = r.wi.shape[0]
    slots = tuple(range(hidden))

    r.wait("x", "wq", "wk", "wv")
    for block in range(blocks):
        cols = rows_of(block)
        xb = r.x[cols]
        r.qt[:, cols] = (dot_tt(r.wq[...], xb) * HEAD_DIM**-0.5).astype(bf16)
        r.kt[:, cols] = dot_tt(r.wk[...], xb).astype(bf16)
        r.vt[:, cols] = dot_tt(r.wv[...], xb).astype(bf16)
    net.tick(At.PROJECT)

    row_at = lax.broadcasted_iota(jnp.int32, (BLOCK, BLOCK), 0)
    col_at = lax.broadcasted_iota(jnp.int32, (BLOCK, BLOCK), 1)
    causal = row_at <= col_at
    away = jnp.where(r.count > 0, 0.0, 2e9).astype(f32)

    def soften(head, qb):
        hs = head_of(head)
        query = r.qt[hs, rows_of(qb)]
        parts = []
        peak_off = None
        for tb in range(qb + 1):
            scores = dot_tn(r.kt[hs, rows_of(tb)], query)
            if tb == qb:
                scores = jnp.where(causal, scores, MASKED)
            parts.append(scores)
            peak = jnp.max(scores, axis=0, keepdims=True)
            if tb < qb:
                peak_off = peak if peak_off is None else jnp.maximum(peak_off, peak)
        if peak_off is not None:
            peak = jnp.maximum(peak, peak_off - away)
        total = jnp.zeros((1, BLOCK), f32)
        for tb in range(qb + 1):
            expo = jnp.exp(parts[tb] - (peak if tb == qb else peak + away))
            total += jnp.sum(expo, axis=0, keepdims=True)
            r.p[qb][head, rows_of(tb)] = expo.astype(bf16)
        r.inv_total[pl.ds(head, 1), rows_of(qb)] = 1.0 / total

    def mix(head, qb):
        hs = head_of(head)
        mixed = dot_nn(r.vt[hs, : (qb + 1) * BLOCK], r.p[qb][head])
        mixed *= r.inv_total[pl.ds(head, 1), rows_of(qb)]
        r.mt[hs, rows_of(qb)] = mixed.astype(bf16)

    for head in range(HEADS + 1):
        for qb in range(blocks):
            if head < HEADS:
                soften(head, qb)
            if head > 0:
                mix(head - 1, qb)
        net.tick(At.ATTEND, head)

    r.wait("wo", "dual")
    gain_one, shift_one = r.gain_one[...][None], r.shift_one[...][None]

    def norm_block(block):
        rows = rows_of(block)
        attended = dot_tn(r.mt[:, rows], r.wo[...])
        r.dual[rows] += attended
        hidden_one = r.x[rows].astype(f32) + attended
        centre = hidden_one - row_mean(hidden_one)
        inverse = lax.rsqrt(row_mean(centre * centre) + EPSILON)
        normed = centre * inverse
        r.n1[rows] = normed
        r.i1[rows] = inverse
        r.fl[rows] = (normed * gain_one + shift_one).astype(bf16)

    each(blocks, norm_block, NORM_UNROLL)

    def half_block(block, pair, place):
        first_low = r.fl[rows_of(block)]
        th, rows = split(block)
        for j in pair:
            pre = dot_nn(first_low, r.wi[j]) + r.bi[j, 0:1]
            phi = 0.5 + 0.5 * lax.erf(pre * 0.7071067811865476)
            bell = jnp.exp(-0.5 * pre * pre) * 0.3989422804014327
            r.act[j, th, rows] = (pre * phi).astype(bf16)
            r.slope[j, th, rows] = (phi + pre * bell).astype(bf16)
        net.loop_tick(place, block, blocks)

    net.tick(At.HIDDEN)
    each(blocks, lambda block: half_block(block, slots[:2], At.HALVES), HALF_UNROLL)
    net.tick(At.OTHERS)
    each(blocks, lambda block: half_block(block, slots[2:], At.HALVES2), HALF_UNROLL)

    r.wait("cm", "cd")
    net.tick(At.BRANCH)
    gain_two, shift_two = r.gain_two[...][None], r.shift_two[...][None]
    bias_out = r.bias_out[...][None]
    r.gvec[...] = jnp.zeros_like(r.gvec)

    def second_block(block):
        rows = rows_of(block)
        th, cut = split(block)
        branch = dot_nn(r.act[0, th, cut], r.wo2[0])
        for j in slots[1:]:
            branch += dot_nn(r.act[j, th, cut], r.wo2[j])
        branch += bias_out
        r.dual[rows] += branch
        hidden_two = r.n1[rows] * gain_one + shift_one + branch
        centre = hidden_two - row_mean(hidden_two)
        inverse = lax.rsqrt(row_mean(centre * centre) + EPSILON)
        normed = centre * inverse
        r.gwi[th, cut] = (normed * gain_two + shift_two).astype(bf16)
        grad = r.cm[rows]
        r.gvec[3:4] += col_sum(grad * normed)
        r.gvec[4:5] += col_sum(grad)
        scaled = grad * gain_two
        g_sum = inverse * (
            scaled - row_mean(scaled) - normed * row_mean(scaled * normed)
        )
        r.cm[rows] = g_sum
        g_branch = (g_sum + r.cd[rows]).astype(bf16)
        r.gb[rows] = g_branch
        r.gvec[2:3] += col_sum(g_branch.astype(f32))

    each(blocks, second_block, SECOND_UNROLL)
    r.put("lo", 0)
    r.put("lo", 1)
    r.put("dual", 0)

    for j in reversed(slots):
        r.gwo2[j] = dot_tn(joined(r.act[j]), r.gb[...]).astype(bf16)
        net.tick(At.OUT, j)
    r.gbi[...] = jnp.zeros_like(r.gbi)

    def pre_block(block):
        g_branch = r.gb[rows_of(block)]
        th, rows = split(block)
        for j in slots:
            g_act = dot_nt(g_branch, r.wo2[j])
            g_pre = (g_act * r.slope[j, th, rows].astype(f32)).astype(bf16)
            r.slope[j, th, rows] = g_pre
            r.gbi[j] += col_sum(g_pre.astype(f32))
        net.loop_tick(At.PRE, block, blocks)

    each(blocks, pre_block, PRE_UNROLL)
    r.finished("lo")
    for j in reversed(slots):
        r.gwi[j] = dot_tn(r.fl[...], joined(r.slope[j])).astype(bf16)
        net.tick(At.IN, j)

    def first_block(block):
        rows = rows_of(block)
        th, cut = split(block)
        g_first = dot_nt(r.slope[0, th, cut], r.wi[0])
        for j in slots[1:]:
            g_first += dot_nt(r.slope[j, th, cut], r.wi[j])
        g_first += r.cm[rows]
        normed = r.n1[rows]
        r.gvec[0:1] += col_sum(g_first * normed)
        r.gvec[1:2] += col_sum(g_first)
        scaled = g_first * gain_one
        g_resid = r.i1[rows] * (
            scaled - row_mean(scaled) - normed * row_mean(scaled * normed)
        )
        r.cm[rows] = g_resid
        g_att = (g_resid + r.cd[rows]).astype(bf16)
        r.gb[rows] = g_att
        g_mixed = dot_nt(r.wo[...], g_att)
        g_mixed = g_mixed.reshape(HEADS, HEAD_DIM, BLOCK) * r.inv_total[:, rows][:, None]
        g_mixed = g_mixed.reshape(width, BLOCK).astype(bf16)
        r.act[3, th, :, cut] = g_mixed
        centred = g_mixed.astype(f32) * r.mt[:, rows].astype(f32)
        r.centred[:, rows] = jnp.sum(centred.reshape(HEADS, HEAD_DIM, BLOCK), axis=1)
        net.loop_tick(At.FIRST, block, blocks)

    each(blocks, first_block, FIRST_UNROLL)
    r.gw[0] = dot_nn(r.mt[...], r.gb[...]).astype(bf16)
    net.tick(At.W_OUTPUT)
    for th in range(2):
        r.slope[0, th] = r.x[th * HALF : (th + 1) * HALF].T

    def columns(which, head, block):
        th, cut = split(block)
        return which, th, head_of(head), cut

    def back_values(head, tb):
        total = None
        for qb in range(tb, blocks):
            part = dot_nt(r.act[columns(3, head, qb)], r.p[qb][head, rows_of(tb)])
            total = part if total is None else total + part
        r.act[columns(2, head, tb)] = total.astype(bf16)

    def back_scores(head, qb, slot):
        got = r.act[columns(3, head, qb)]
        centred = r.centred[pl.ds(head, 1), rows_of(qb)]
        for tb in range(qb + 1):
            g_probs = dot_tn(r.vt[head_of(head), rows_of(tb)], got)
            probs = r.p[qb][head, rows_of(tb)].astype(f32)
            slot[qb][rows_of(tb)] = (probs * (g_probs - centred)).astype(bf16)

    def back_query(head, qb, slot):
        g_query = dot_nn(r.kt[head_of(head), : (qb + 1) * BLOCK], slot[qb][...])
        r.act[columns(0, head, qb)] = (g_query * HEAD_DIM**-0.5).astype(bf16)

    def back_keys(head, tb, slot):
        total = None
        for qb in range(tb, blocks):
            part = dot_nt(r.qt[head_of(head), rows_of(qb)], slot[qb][rows_of(tb)])
            total = part if total is None else total + part
        r.act[columns(1, head, tb)] = total.astype(bf16)

    def against_x(which, rows):
        total = dot_nt(r.slope[0, 0], r.act[which, 0, rows])
        return (total + dot_nt(r.slope[0, 1], r.act[which, 1, rows])).astype(bf16)

    for head in range(HEADS):
        for tb in range(blocks):
            back_values(head, tb)
        net.tick(At.VALUES, head)
    r.gw[1] = against_x(2, slice(0, width))
    net.tick(At.W_VALUE)
    size = HEADS // PARTS
    part_width = size * HEAD_DIM

    for head in range(HEADS + 1):
        for block in range(blocks):
            if head < HEADS:
                back_scores(head, block, r.gs[head % 2])
            if head > 0:
                back_query(head - 1, block, r.gs[(head - 1) % 2])
                back_keys(head - 1, block, r.gs[(head - 1) % 2])
        if head > 0 and head % size == 0:
            part = head // size - 1
            rows = span_of(part, part_width)
            r.gqk[part, :, :part_width] = against_x(0, rows)
            r.gqk[part, :, part_width:] = against_x(1, rows)
        net.tick(At.SCORES, head)

    def input_block(block):
        rows = rows_of(block)
        th, cut = split(block)
        grad = dot_tt(r.act[0, th, :, cut], r.wq[...])
        grad += dot_tt(r.act[1, th, :, cut], r.wk[...])
        grad += dot_tt(r.act[2, th, :, cut], r.wv[...])
        r.cm[rows] += grad
        net.loop_tick(At.INPUT, block, blocks)

    each(blocks, input_block, INPUT_UNROLL)
    r.put("cm", 0)
    net.tick(At.END)


class Refs:
    def __init__(self, names, refs):
        self.__dict__.update(zip(names, refs))
        self.pending = {}
        self.out = {}

    def fetch(self, name, source, target, sem):
        copy = pltpu.make_async_copy(source, target, sem)
        copy.start()
        self.pending[name] = copy

    def wait(self, *names):
        for name in names:
            self.pending.pop(name).wait()

    def put(self, name, at):
        source, target, sem = self.outs[name, at]
        copy = pltpu.make_async_copy(source, target, sem)
        copy.start()
        self.out[name, at] = copy

    def finished(self, name):
        for key in [key for key in self.out if key[0] == name]:
            self.out.pop(key).wait()

    def drain(self):
        for copy in self.out.values():
            copy.wait()


FETCHED = ("x", "wq", "wk", "wv", "wo", "dual", "cm", "cd")


def scratch_of(tokens, width, hidden):
    vmem = pltpu.VMEM
    wide = (hidden, tokens // HALF, HALF, HALF)
    names = dict(
        x=vmem((tokens, width), bf16),
        wq=vmem((width, width), bf16),
        wk=vmem((width, width), bf16),
        wv=vmem((width, width), bf16),
        wo=vmem((width, width), bf16),
        dual=vmem((tokens, width), f32),
        cm=vmem((tokens, width), f32),
        cd=vmem((tokens, width), f32),
        qt=vmem((width, tokens), bf16),
        kt=vmem((width, tokens), bf16),
        vt=vmem((width, tokens), bf16),
        mt=vmem((width, tokens), bf16),
        inv_total=vmem((HEADS, tokens), f32),
        centred=vmem((HEADS, tokens), f32),
        n1=vmem((tokens, width), f32),
        i1=vmem((tokens, 1), f32),
        fl=vmem((tokens, width), bf16),
        act=vmem(wide, bf16),
        slope=vmem(wide, bf16),
        gb=vmem((tokens, width), bf16),
    )
    for qb in range(tokens // BLOCK):
        names[f"p{qb}"] = vmem((HEADS, (qb + 1) * BLOCK, BLOCK), bf16)
        names[f"g{qb}"] = vmem(((qb + 1) * BLOCK, BLOCK), bf16)
        names[f"h{qb}"] = vmem(((qb + 1) * BLOCK, BLOCK), bf16)
    return names


def begin(r, tokens):
    blocks = tokens // BLOCK
    r.count = r.count_ref[0]
    r.p = [getattr(r, f"p{qb}") for qb in range(blocks)]
    r.gs = [[getattr(r, f"{s}{qb}") for qb in range(blocks)] for s in "gh"]
    for at, name in enumerate(FETCHED):
        r.fetch(name, getattr(r, name + "_hbm"), getattr(r, name), r.sems.at[at])
    base = len(FETCHED)
    r.outs = {
        ("lo", 0): (r.gwi.at[0], r.lo_out.at[0:HALF], r.sems.at[base]),
        ("lo", 1): (r.gwi.at[1], r.lo_out.at[HALF : 2 * HALF], r.sems.at[base + 1]),
        ("dual", 0): (r.dual, r.dual_out, r.sems.at[base + 2]),
        ("cm", 0): (r.cm, r.gx_out, r.sems.at[base + 3]),
    }
    return base + 4


class Quiet:
    def tick(self, *place):
        pass

    def loop_tick(self, place, at, count):
        pass


class At:
    (PROJECT, ATTEND, HIDDEN, HALVES, OTHERS, HALVES2, BRANCH, OUT, PRE, IN, FIRST, W_OUTPUT,
     VALUES, W_VALUE, SCORES, INPUT, END) = range(17)


class Kind:
    (W_X, W_Y, W_CORE, W_PASS, W_TURN, W_BIAS, F_AWAY, F_NEAR, F_X, F_Y, F_Y_OWN, F_NEXT, F_FAR,
     G_FAR, G_Y, G_NEXT, A_CORE, A_ONE, A_TWO, A_NEXT, A_FAR, B_FAR, B_NEXT, B_TWO, B_ONE, B_CORE,
     V_STEP) = range(27)


class Net:
    def __init__(self, r, plan):
        self.r = r
        self.plan = plan
        b, w = lax.axis_index("batch"), lax.axis_index("wide")
        z, y, x, c = b // 2, b % 2, w // 2, w % 2
        self.y, self.x, self.c, self.w = y, x, c, w
        self.core = (b, x * 2 + 1 - c)
        self.ex = (b, (1 - x) * 2 + c)
        self.diagonal = (b, (1 - x) * 2 + 1 - c)
        self.why = (z * 2 + 1 - y, w)
        self.odd, self.high = z % 2, z // 2
        self.next = ((z + 1 - 2 * self.odd) * 2 + y, w)
        self.far = (((z + 2) % 4) * 2 + y, w)
        self.table = {}
        self.used = set()
        self.parts = []
        self.describe()

    def copy(self, name, to, source, target):
        self.table[name] = (len(self.table), to, source, target)

    def build(self, name):
        index, to, source, target = self.table[name]
        return pltpu.make_async_remote_copy(
            src_ref=source(),
            dst_ref=target(),
            send_sem=self.r.send_sem.at[index],
            recv_sem=self.r.recv_sem.at[index],
            device_id=to,
            device_id_type=pl.DeviceIdType.MESH,
        )

    def start(self, *names):
        for name in names:
            self.used.add(name)
            self.build(name).start()

    def got(self, *names):
        for name in names:
            self.build(name).wait_recv()

    def tick(self, *place):
        for event, *args in self.plan.get(place, ()):
            event(self, *args)

    def loop_tick(self, place, at, count):
        for k in range(count):
            if self.plan.get((place, k)):
                self.guard(at, k, place)

    def guard(self, at, k, place):
        if isinstance(at, int):
            if at == k:
                self.tick(place, k)
        else:
            pl.when(at == k)(functools.partial(self.tick, place, k))

    def span(self, start, size):
        return pl.ds(pl.multiple_of(start, size), size)

    def describe(self):
        r, copy, span = self.r, self.copy, self.span
        y, x, c, odd, high = self.y, self.x, self.c, self.odd, self.high
        own = (r.wi_hbm, r.wo2_hbm)
        held = (r.wi, r.wo2)
        for m in range(2):
            copy((Kind.W_CORE, m), self.core, lambda m=m: own[m], lambda m=m: held[m].at[1])
            for q in range(2):
                mine = lambda q=q: span(y * 256 + q * 128, 128)
                other = lambda q=q: span((1 - y) * 256 + q * 128, 128)
                copy((Kind.W_X, m, q), self.ex, lambda m=m, f=mine: own[m].at[f()], lambda m=m, f=mine: held[m].at[2, f()])
                copy((Kind.W_Y, m, q), self.why, lambda m=m, f=mine: held[m].at[2, f()], lambda m=m, f=mine: held[m].at[2, f()])
                copy((Kind.W_PASS, m, q), self.core, lambda m=m, f=mine: held[m].at[2, f()], lambda m=m, f=mine: held[m].at[3, f()])
                copy((Kind.W_TURN, m, q), self.core, lambda m=m, f=other: held[m].at[2, f()], lambda m=m, f=other: held[m].at[3, f()])
        for slot, to in ((1, self.core), (2, self.ex), (3, self.diagonal)):
            copy((Kind.W_BIAS, slot), to, lambda: r.bi.at[0], lambda slot=slot: r.bi.at[slot])

        grads = (r.gwo2, r.gwi)
        for m in range(2):
            copy((Kind.F_AWAY, m), self.core, lambda m=m: grads[m].at[3], lambda m=m: r.rca.at[m])
            copy((Kind.F_NEAR, m), self.core, lambda m=m: grads[m].at[1], lambda m=m: r.rcd.at[m])
            for h in range(2):
                kept = lambda h=h: span(h * 256 + y * 128, 128)
                away = lambda h=h: span(h * 256 + (1 - y) * 128, 128)
                if h == 0:
                    copy((Kind.F_X, m, h), self.ex, lambda m=m: grads[m].at[2, 0:256], lambda m=m: r.rx.at[m, 0:256])
                else:
                    copy((Kind.F_X, m, h), self.ex, lambda m=m, f=kept: grads[m].at[2, f()], lambda m=m: r.rx.at[m, 256:384])
                    copy((Kind.F_Y_OWN, m, h), self.why, lambda m=m, f=away: grads[m].at[0, f()], lambda m=m: r.ry.at[m, 2])
                slot = 0 if h == 0 else 2
                copy((Kind.F_Y, m, h), self.why, lambda m=m, s=slot, f=away: grads[m].at[s, f()], lambda m=m, h=h: r.ry.at[m, h])
                u = m * 2 + h
                near = lambda h=h: span(h * 256 + y * 128 + odd * 64, 64)
                near_y = lambda h=h: span(h * 256 + (1 - y) * 128 + odd * 64, 64)
                gone = lambda h=h: span(h * 256 + y * 128 + (1 - odd) * 64, 64)
                piece = lambda h=h: span(h * 256 + y * 128 + odd * 64 + high * 32, 32)
                gone2 = lambda h=h: span(h * 256 + y * 128 + odd * 64 + (1 - high) * 32, 32)
                copy((Kind.F_NEXT, m, h), self.next, lambda m=m, f=gone: grads[m].at[0, f()], lambda u=u: r.rn.at[u])
                copy((Kind.F_FAR, m, h), self.far, lambda m=m, f=gone2: grads[m].at[0, f()], lambda u=u: r.rf.at[u])
                for kind, to, rows in ((Kind.G_FAR, self.far, piece), (Kind.G_Y, self.why, near)):
                    copy((kind, m, h), to, lambda m=m, f=rows: r.fout.at[m, f()], lambda m=m, f=rows: r.fout.at[m, f()])
                for k, rows in enumerate((near, near_y)):
                    copy((Kind.G_NEXT, m, h, k), self.next, lambda m=m, f=rows: r.fout.at[m, f()], lambda m=m, f=rows: r.fout.at[m, f()])

        for n in range(2 + PARTS):
            refs = (r.gw, r.ac, r.a1, r.a2, r.a3, r.a4, r.aout)
            at = n
            if n >= 2:
                refs = (r.gqk, r.qc, r.q1, r.q2, r.q3, r.q4, r.qout)
                at = n - 2
            grad, *received, out = [ref.at[at] for ref in refs]
            first, second = ((self.ex, x), (self.why, y))
            if Y_FIRST[n]:
                first, second = second, first
            levels = ((self.core, c), first, second, (self.next, odd), (self.far, high))
            kinds = (Kind.A_CORE, Kind.A_ONE, Kind.A_TWO, Kind.A_NEXT, Kind.A_FAR)
            back = (Kind.B_CORE, Kind.B_ONE, Kind.B_TWO, Kind.B_NEXT, Kind.B_FAR)
            size = grad.shape[0]
            base = lambda: 0
            keeps = []
            for level, (to, bit) in enumerate(levels):
                size //= 2
                keep = lambda f=base, p=bit, s=size: span(f() + p * s, s)
                give = lambda f=base, p=bit, s=size: span(f() + (1 - p) * s, s)
                base = lambda f=base, p=bit, s=size: f() + p * s
                keeps.append(keep)
                copy((kinds[level], n), to, lambda g=grad, f=give: g.at[f()], lambda t=received[level]: t)
                copy((back[level], n), to, lambda o=out, f=keep: o.at[f()], lambda o=out, f=keep: o.at[f()])
            self.parts.append((grad, received, out, keeps))

        for at, to in enumerate((self.core, self.ex, self.why, self.next, self.far)):
            copy((Kind.V_STEP, at), to, lambda at=at: r.vs.at[at], lambda at=at: r.vr.at[at])

    def enter(self):
        barrier = pltpu.get_barrier_semaphore()
        peers = [self.core, self.ex, self.diagonal, self.why, self.next, self.far]
        for peer in peers:
            pl.semaphore_signal(barrier, inc=1, device_id=peer, device_id_type=pl.DeviceIdType.MESH)
        pl.semaphore_wait(barrier, len(peers))
        for slot in (1, 2, 3):
            self.start((Kind.W_BIAS, slot))
        for m in range(2):
            self.start((Kind.W_X, m, 0), (Kind.W_X, m, 1))
        self.start((Kind.W_CORE, 0), (Kind.W_CORE, 1))

    def pass_x(self, m, q):
        self.got((Kind.W_X, m, q))
        self.start((Kind.W_Y, m, q), (Kind.W_PASS, m, q))

    def pass_y(self, m, q):
        self.got((Kind.W_Y, m, q))
        self.start((Kind.W_TURN, m, q))

    def arrived_near(self, m):
        if m == 0:
            self.got((Kind.W_BIAS, 1), (Kind.W_BIAS, 2), (Kind.W_BIAS, 3))
        self.got((Kind.W_CORE, m))

    def arrived_far(self, m):
        for q in range(2):
            self.got((Kind.W_PASS, m, q), (Kind.W_TURN, m, q))

    def grad(self, m):
        return (self.r.gwo2, self.r.gwi)[m]

    def f_core(self, m, slot):
        self.start((Kind.F_AWAY if slot == 3 else Kind.F_NEAR, m))

    def f_x(self, m):
        r, grad = self.r, self.grad(m)
        self.got((Kind.F_AWAY, m))
        grad[2] = (grad[2].astype(f32) + r.rca[m].astype(f32)).astype(bf16)
        self.start((Kind.F_X, m, 0), (Kind.F_Y, m, 1))

    def f_near(self, m):
        r, grad = self.r, self.grad(m)
        self.got((Kind.F_NEAR, m))
        grad[0] = (grad[0].astype(f32) + r.rcd[m].astype(f32)).astype(bf16)
        self.start((Kind.F_Y_OWN, m, 1))

    def f_own(self, m, h):
        r, grad = self.r, self.grad(m)
        y = self.y
        if h == 0:
            self.got((Kind.F_X, m, 0))
            total = grad[0, 0:256].astype(f32) + r.rx[m, 0:256].astype(f32)
            grad[0, 0:256] = total.astype(bf16)
            self.start((Kind.F_Y, m, 0))
        else:
            self.got((Kind.F_Y, m, 1))
            s = self.span(256 + y * 128, 128)
            grad[2, s] = (grad[2, s].astype(f32) + r.ry[m, 1].astype(f32)).astype(bf16)
            self.start((Kind.F_X, m, 1))

    def f_y(self, m, h):
        r, grad = self.r, self.grad(m)
        s = self.span(h * 256 + self.y * 128, 128)
        if h == 0:
            self.got((Kind.F_Y, m, 0))
            total = grad[0, s].astype(f32) + r.ry[m, 0].astype(f32)
        else:
            self.got((Kind.F_Y_OWN, m, 1), (Kind.F_X, m, 1))
            total = grad[0, s].astype(f32) + r.ry[m, 2].astype(f32) + r.rx[m, 256:384].astype(f32)
        grad[0, s] = total.astype(bf16)
        self.start((Kind.F_NEXT, m, h))

    def f_z(self, m, h):
        r, grad = self.r, self.grad(m)
        self.got((Kind.F_NEXT, m, h))
        s = self.span(h * 256 + self.y * 128 + self.odd * 64, 64)
        grad[0, s] = (grad[0, s].astype(f32) + r.rn[m * 2 + h].astype(f32)).astype(bf16)
        self.start((Kind.F_FAR, m, h))

    def f_zz(self, m, h):
        r, grad = self.r, self.grad(m)
        self.got((Kind.F_FAR, m, h))
        s = self.span(h * 256 + self.y * 128 + self.odd * 64 + self.high * 32, 32)
        r.fout[m, s] = (grad[0, s].astype(f32) + r.rf[m * 2 + h].astype(f32)).astype(bf16)
        self.start((Kind.G_FAR, m, h))

    def f_g(self, m, h):
        self.got((Kind.G_FAR, m, h))
        self.start((Kind.G_Y, m, h), (Kind.G_NEXT, m, h, 0))

    def f_gg(self, m, h):
        self.got((Kind.G_Y, m, h))
        self.start((Kind.G_NEXT, m, h, 1))

    def f_end(self, m, h):
        self.got((Kind.G_NEXT, m, h, 0), (Kind.G_NEXT, m, h, 1))
        self.r.put("f", m * 2 + h)

    def a_core(self, n):
        self.start((Kind.A_CORE, n))

    def a_sum(self, n, level, target=None):
        grad, received, _, keeps = self.parts[n]
        s = keeps[level]()
        total = grad[s].astype(f32) + received[level][...].astype(f32)
        (grad if target is None else target)[s] = total.astype(bf16)

    def a_1(self, n):
        self.got((Kind.A_CORE, n))
        self.a_sum(n, 0)
        self.start((Kind.A_ONE, n))

    def a_2(self, n):
        self.got((Kind.A_ONE, n))
        self.a_sum(n, 1)
        self.start((Kind.A_TWO, n))

    def a_z(self, n):
        self.got((Kind.A_TWO, n))
        self.a_sum(n, 2)
        self.start((Kind.A_NEXT, n))

    def a_zz(self, n):
        self.got((Kind.A_NEXT, n))
        self.a_sum(n, 3)
        self.start((Kind.A_FAR, n))

    def a_g(self, n):
        self.got((Kind.A_FAR, n))
        self.a_sum(n, 4, self.parts[n][2])
        self.start((Kind.B_FAR, n))

    def a_gg(self, n):
        self.got((Kind.B_FAR, n))
        self.start((Kind.B_NEXT, n))

    def a_3(self, n):
        self.got((Kind.B_NEXT, n))
        self.start((Kind.B_TWO, n))

    def a_4(self, n):
        self.got((Kind.B_TWO, n))
        self.start((Kind.B_ONE, n))

    def a_5(self, n):
        self.got((Kind.B_ONE, n))
        self.start((Kind.B_CORE, n))

    def a_end(self, n):
        self.got((Kind.B_CORE, n))
        self.r.put("a", n)

    def v_core(self):
        r = self.r
        x, c = self.x, self.c
        r.vs[0, 0:8] = r.gvec[...]
        r.vs[0, pl.ds(8 + x * 2 + c, 1)] = r.gbi[0]
        r.vs[0, pl.ds(8 + x * 2 + 1 - c, 1)] = r.gbi[1]
        r.vs[0, pl.ds(8 + (1 - x) * 2 + c, 1)] = r.gbi[2]
        r.vs[0, pl.ds(8 + (1 - x) * 2 + 1 - c, 1)] = r.gbi[3]
        self.start((Kind.V_STEP, 0))

    def v_next(self, at):
        r = self.r
        self.got((Kind.V_STEP, at))
        r.vs[at + 1] = r.vs[at] + r.vr[at]
        if at < 4:
            self.start((Kind.V_STEP, at + 1))
        else:
            r.vs[5, 12:13] = r.vs[5, pl.ds(8 + self.w, 1)]
            r.put("v", 0)

    def leave(self):
        for name in self.table:
            if name in self.used:
                self.build(name).wait_send()


def plain_kernel(names, *refs):
    r = Refs(names, refs)
    begin(r, r.x.shape[0])
    layer(r, Quiet())
    r.drain()


ANY = pl.BlockSpec(memory_space=pl.ANY)
IN_VMEM = pl.BlockSpec(memory_space=pltpu.VMEM)
IN_SMEM = pl.BlockSpec(memory_space=pltpu.SMEM)
COST = pl.CostEstimate(
    flops=25 * 10**9, bytes_accessed=30 << 20, transcendentals=12 << 20
)


def plain_layer(operands, count, vectors, wi, bi, wo2):
    tokens, width = operands["x_hbm"].shape
    hidden = wi.shape[0]
    shape = jax.ShapeDtypeStruct
    ins = {name: (value, ANY) for name, value in operands.items()}
    ins.update(count_ref=(count, IN_SMEM))
    ins.update({name: (value, IN_VMEM) for name, value in vectors.items()})
    ins.update(wi=(wi, IN_VMEM), bi=(bi, IN_VMEM), wo2=(wo2, IN_VMEM))
    outs = dict(
        lo_out=(shape((tokens, width), bf16), ANY),
        dual_out=(shape((tokens, width), f32), ANY),
        gx_out=(shape((tokens, width), f32), ANY),
        gw=(shape((2, width, width), bf16), IN_VMEM),
        gqk=(shape((PARTS, width, 2 * width // PARTS), bf16), IN_VMEM),
        gwi=(shape((hidden, width, HALF), bf16), IN_VMEM),
        gwo2=(shape((hidden, HALF, width), bf16), IN_VMEM),
        gvec=(shape((8, width), f32), IN_VMEM),
        gbi=(shape((hidden, 1, HALF), f32), IN_VMEM),
    )
    scratch = scratch_of(tokens, width, hidden)
    scratch["sems"] = pltpu.SemaphoreType.DMA((len(FETCHED) + 4,))
    names = list(ins) + list(outs) + list(scratch)
    return pl.pallas_call(
        functools.partial(plain_kernel, names),
        out_shape=[o[0] for o in outs.values()],
        in_specs=[i[1] for i in ins.values()],
        out_specs=[o[1] for o in outs.values()],
        scratch_shapes=list(scratch.values()),
        compiler_params=pltpu.CompilerParams(vmem_limit_bytes=62 << 20),
        cost_estimate=COST,
    )(*[i[0] for i in ins.values()])


def sort_out(layer_in, dual_in, long_count, w_query, w_key, w_value, w_output, gain_one, shift_one,
             w_in, bias_in, w_out, bias_out, gain_two, shift_two, cot_main, cot_dual):
    operands = dict(
        x_hbm=layer_in, wq_hbm=w_query, wk_hbm=w_key, wv_hbm=w_value, wo_hbm=w_output,
        dual_hbm=dual_in, cm_hbm=cot_main, cd_hbm=cot_dual,
    )
    vectors = dict(
        gain_one=gain_one, shift_one=shift_one, gain_two=gain_two, shift_two=shift_two, bias_out=bias_out
    )
    return operands, long_count, vectors, w_in, bias_in, w_out


def plain_body(*args):
    operands, count, vectors, w_in, bias_in, w_out = sort_out(*args)
    width = w_in.shape[0]
    w_in_all = lax.all_gather(w_in, "wide", axis=1, tiled=True)
    bias_all = lax.all_gather(bias_in, "wide", axis=0, tiled=True)
    w_out_all = lax.all_gather(w_out, "wide", axis=0, tiled=True)
    hidden = w_in_all.shape[1] // HALF
    wi = w_in_all.reshape(width, hidden, HALF).transpose(1, 0, 2)
    wo2 = w_out_all.reshape(hidden, HALF, width)
    bi = bias_all.astype(f32).reshape(hidden, 1, HALF)
    lo, dual, gx, gw, gqk, gwi, gwo2, gvec, gbi = plain_layer(operands, count, vectors, wi, bi, wo2)
    gwi = gwi.transpose(1, 0, 2).reshape(w_in_all.shape)
    gwo2 = gwo2.reshape(w_out_all.shape)
    gwi = lax.psum(lax.psum_scatter(gwi, "wide", scatter_dimension=1, tiled=True), "batch")
    gwo2 = lax.psum(lax.psum_scatter(gwo2, "wide", scatter_dimension=0, tiled=True), "batch")
    gbi = lax.psum_scatter(gbi.reshape(-1), "wide", scatter_dimension=0, tiled=True)
    gbi = lax.psum(gbi, "batch")
    gw, gqk, gvec = lax.psum((gw, gqk, gvec), ("batch", "wide"))
    gw, gqk = gw.astype(f32), gqk.astype(f32)
    part = width // PARTS
    gq = jnp.concatenate(list(gqk[:, :, :part]), axis=1)
    gk = jnp.concatenate(list(gqk[:, :, part:]), axis=1)
    return (lo, dual, gx, gq, gk, gw[1], gw[0], gvec[0], gvec[1], gwi.astype(f32), gbi,
            gwo2.astype(f32), gvec[2], gvec[3], gvec[4])


def steps():
    n = Net
    plan = {}
    plan[(At.ATTEND, 0)] = (
        (n.pass_x, 0, 0),
    )
    plan[(At.ATTEND, 5)] = (
        (n.pass_x, 0, 1),
    )
    plan[(At.ATTEND, 8)] = (
        (n.pass_y, 0, 0),
    )
    plan[(At.HIDDEN,)] = (
        (n.pass_x, 1, 0),
        (n.arrived_near, 0),
    )
    plan[(At.HALVES, 3)] = (
        (n.pass_y, 0, 1),
        (n.pass_x, 1, 1),
    )
    plan[(At.OTHERS,)] = (
        (n.pass_y, 1, 0),
        (n.arrived_far, 0),
    )
    plan[(At.BRANCH,)] = (
        (n.pass_y, 1, 1),
        (n.arrived_near, 1),
        (n.arrived_far, 1),
    )
    plan[(At.OUT, 3)] = (
        (n.f_core, 0, 3),
    )
    plan[(At.OUT, 1)] = (
        (n.f_core, 0, 1),
    )
    plan[(At.PRE, 1)] = (
        (n.f_x, 0),
        (n.f_near, 0),
    )
    plan[(At.IN, 3)] = (
        (n.f_core, 1, 3),
    )
    plan[(At.IN, 1)] = (
        (n.f_core, 1, 1),
    )
    plan[(At.FIRST, 1)] = (
        (n.f_x, 1),
        (n.f_own, 0, 1),
        (n.f_near, 1),
        (n.f_own, 0, 0),
    )
    plan[(At.W_OUTPUT,)] = (
        (n.a_core, 0),
        (n.v_core,),
    )
    plan[(At.VALUES, 1)] = (
        (n.f_own, 1, 1),
    )
    plan[(At.VALUES, 4)] = (
        (n.v_next, 0),
        (n.a_1, 0),
    )
    plan[(At.W_VALUE,)] = (
        (n.a_core, 1),
        (n.f_own, 1, 0),
    )
    plan[(At.SCORES, 1)] = (
        (n.a_1, 1),
        (n.f_y, 0, 0),
        (n.f_y, 0, 1),
    )
    plan[(At.SCORES, 2)] = (
        (n.a_core, 2),
    )
    plan[(At.SCORES, 3)] = (
        (n.a_2, 0),
        (n.f_y, 1, 1),
        (n.v_next, 1),
        (n.a_1, 2),
    )
    plan[(At.SCORES, 4)] = (
        (n.a_core, 3),
        (n.f_z, 0, 0),
    )
    plan[(At.SCORES, 5)] = (
        (n.f_z, 0, 1),
        (n.f_y, 1, 0),
        (n.a_z, 0),
        (n.a_1, 3),
        (n.f_z, 1, 1),
    )
    plan[(At.SCORES, 6)] = (
        (n.a_core, 4),
        (n.a_2, 1),
    )
    plan[(At.SCORES, 7)] = (
        (n.f_zz, 0, 0),
        (n.v_next, 2),
    )
    plan[(At.SCORES, 8)] = (
        (n.a_core, 5),
        (n.a_1, 4),
        (n.a_2, 3),
        (n.a_2, 2),
        (n.a_zz, 0),
        (n.f_zz, 0, 1),
        (n.a_z, 1),
        (n.f_z, 1, 0),
    )
    plan[(At.INPUT, 1)] = (
        (n.f_zz, 1, 1),
        (n.v_next, 3),
        (n.a_1, 5),
    )
    plan[(At.INPUT, 3)] = (
        (n.a_2, 4),
        (n.a_z, 3),
        (n.a_g, 0),
        (n.a_z, 2),
        (n.a_zz, 1),
        (n.f_g, 0, 0),
    )
    plan[(At.END,)] = (
        (n.f_g, 0, 1),
        (n.a_2, 5),
        (n.a_z, 4),
        (n.a_zz, 3),
        (n.f_zz, 1, 0),
        (n.a_zz, 2),
        (n.f_gg, 0, 0),
        (n.f_g, 1, 1),
        (n.f_gg, 0, 1),
        (n.v_next, 4),
        (n.a_z, 5),
        (n.a_gg, 0),
        (n.a_zz, 4),
        (n.a_g, 1),
        (n.a_g, 3),
        (n.f_gg, 1, 1),
        (n.f_g, 1, 0),
        (n.a_g, 2),
        (n.f_end, 0, 0),
        (n.a_g, 4),
        (n.a_gg, 1),
        (n.a_gg, 3),
        (n.f_gg, 1, 0),
        (n.a_gg, 2),
        (n.f_end, 0, 1),
        (n.a_zz, 5),
        (n.a_gg, 4),
        (n.a_3, 0),
        (n.f_end, 1, 1),
        (n.a_g, 5),
        (n.a_4, 0),
        (n.a_3, 1),
        (n.a_3, 3),
        (n.a_gg, 5),
        (n.f_end, 1, 0),
        (n.a_3, 2),
        (n.a_3, 4),
        (n.a_3, 5),
        (n.a_4, 1),
        (n.a_5, 0),
        (n.a_4, 3),
        (n.a_4, 2),
        (n.a_4, 4),
        (n.a_end, 0),
        (n.a_4, 5),
        (n.a_5, 3),
        (n.a_5, 1),
        (n.a_5, 4),
        (n.a_end, 3),
        (n.a_5, 2),
        (n.a_5, 5),
        (n.a_end, 1),
        (n.a_end, 4),
        (n.a_end, 2),
        (n.a_end, 5),
    )
    return plan


COPIES = 144


def tuned_kernel(names, *refs):
    r = Refs(names, refs)
    base = begin(r, r.x.shape[0])
    sems = r.sems
    for u in range(4):
        m, cut = u // 2, slice(u % 2 * 256, u % 2 * 256 + 256)
        r.outs["f", u] = (r.fout.at[m, cut], r.f_out.at[m, cut], sems.at[base + u])
    for n in range(2 + PARTS):
        pair = (r.aout.at[n], r.a_out.at[n]) if n < 2 else (r.qout.at[n - 2], r.q_out.at[n - 2])
        r.outs["a", n] = (*pair, sems.at[base + 4 + n])
    r.outs["v", 0] = (r.vs.at[5], r.v_out, sems.at[base + 6 + PARTS])
    r.fetch("wi", r.wi_hbm, r.wi.at[0], sems.at[base + 7 + PARTS])
    r.fetch("wo2", r.wo2_hbm, r.wo2.at[0], sems.at[base + 8 + PARTS])
    r.bi[0] = jnp.broadcast_to(r.bias_in[...].astype(f32)[None], r.bi.shape[1:])
    net = Net(r, steps())
    net.enter()
    r.wait("wi", "wo2")
    layer(r, net)
    net.leave()
    r.drain()


def tuned_layer(operands, count, vectors, w_in, bias_in, w_out):
    tokens, width = operands["x_hbm"].shape
    hidden = 4
    part = 2 * width // PARTS
    shape = jax.ShapeDtypeStruct
    vmem = pltpu.VMEM
    ins = {name: (value, ANY) for name, value in operands.items()}
    ins.update(count_ref=(count, IN_SMEM))
    ins.update({name: (value, IN_VMEM) for name, value in vectors.items()})
    ins.update(wi_hbm=(w_in, ANY), wo2_hbm=(w_out, ANY), bias_in=(bias_in, IN_VMEM))
    outs = dict(
        lo_out=shape((tokens, width), bf16),
        dual_out=shape((tokens, width), f32),
        gx_out=shape((tokens, width), f32),
        f_out=shape((2, HALF, width), bf16),
        a_out=shape((2, width, width), bf16),
        q_out=shape((PARTS, width, part), bf16),
        v_out=shape((16, width), f32),
    )
    scratch = scratch_of(tokens, width, hidden)
    scratch.update(
        wi=vmem((hidden, width, HALF), bf16),
        wo2=vmem((hidden, HALF, width), bf16),
        bi=vmem((hidden, 8, HALF), f32),
        gw=vmem((2, width, width), bf16),
        gqk=vmem((PARTS, width, part), bf16),
        gwi=vmem((hidden, width, HALF), bf16),
        gwo2=vmem((hidden, HALF, width), bf16),
        gvec=vmem((8, width), f32),
        gbi=vmem((hidden, 1, HALF), f32),
        rca=vmem((2, HALF, width), bf16),
        rcd=vmem((2, HALF, width), bf16),
        rx=vmem((2, 384, width), bf16),
        ry=vmem((2, 3, 128, width), bf16),
        rn=vmem((4, 64, width), bf16),
        rf=vmem((4, 32, width), bf16),
        fout=vmem((2, HALF, width), bf16),
        ac=vmem((2, 256, width), bf16),
        a1=vmem((2, 128, width), bf16),
        a2=vmem((2, 64, width), bf16),
        a3=vmem((2, 32, width), bf16),
        a4=vmem((2, 16, width), bf16),
        aout=vmem((2, width, width), bf16),
        qc=vmem((PARTS, 256, part), bf16),
        q1=vmem((PARTS, 128, part), bf16),
        q2=vmem((PARTS, 64, part), bf16),
        q3=vmem((PARTS, 32, part), bf16),
        q4=vmem((PARTS, 16, part), bf16),
        qout=vmem((PARTS, width, part), bf16),
        vs=vmem((6, 16, width), f32),
        vr=vmem((5, 16, width), f32),
        sems=pltpu.SemaphoreType.DMA((len(FETCHED) + 4 + 9 + PARTS,)),
        send_sem=pltpu.SemaphoreType.DMA((COPIES,)),
        recv_sem=pltpu.SemaphoreType.DMA((COPIES,)),
    )
    names = list(ins) + list(outs) + list(scratch)
    return pl.pallas_call(
        functools.partial(tuned_kernel, names),
        out_shape=list(outs.values()),
        in_specs=[i[1] for i in ins.values()],
        out_specs=[ANY] * len(outs),
        scratch_shapes=list(scratch.values()),
        compiler_params=pltpu.CompilerParams(
            vmem_limit_bytes=int(63.5 * 2**20), collective_id=0, has_side_effects=True
        ),
        cost_estimate=COST,
    )(*[i[0] for i in ins.values()])


def widen_kernel(lo, dual, gx, f, a, q, v, lo_out, dual_out, gx_out, gq, gk, gv, go, gwi, gwo,
                 gg1, gs1, gbi, gbo, gg2, gs2, f_low, a_low, q_low, lo_held, dual_held, gx_held, wide, sems):
    loads = ((f, f_low), (a, a_low), (q, q_low), (dual, dual_held), (gx, gx_held), (lo, lo_held))
    copies = []
    for at, (source, target) in enumerate(loads):
        copies.append(pltpu.make_async_copy(source, target, sems.at[at]))
        copies[at].start()
    for at, out in enumerate((gg1, gs1, gbo, gg2, gs2)):
        out[...] = v[at]
    gbi[...] = v[12]
    outs = []

    def send(source, target):
        copy = pltpu.make_async_copy(source, target, sems.at[6 + len(outs)])
        copy.start()
        outs.append(copy)

    copies[0].wait()
    wide[0] = f_low[0].astype(f32)
    send(wide.at[0], gwo)
    wide[1] = f_low[1].astype(f32)
    send(wide.at[1], gwi)
    copies[1].wait()
    wide[2] = a_low[0].astype(f32)
    send(wide.at[2], go)
    wide[3] = a_low[1].astype(f32)
    send(wide.at[3], gv)
    copies[2].wait()
    part = q.shape[2] // 2
    for at, target in ((4, gq), (5, gk)):
        for p in range(PARTS):
            wide[at, :, p * part : (p + 1) * part] = q_low[p, :, (at - 4) * part : (at - 3) * part].astype(f32)
        send(wide.at[at], target)
    for at, source, target in ((3, dual_held, dual_out), (4, gx_held, gx_out), (5, lo_held, lo_out)):
        copies[at].wait()
        send(source, target)
    for copy in outs:
        copy.wait()


def widen(lo, dual, gx, f, a, q, v):
    width = f.shape[2]
    shape = jax.ShapeDtypeStruct
    matrix = (shape((width, width), f32), ANY)
    vector = (shape((width,), f32), IN_VMEM)
    outs = [(shape(t.shape, t.dtype), ANY) for t in (lo, dual, gx)] + [matrix] * 6 + [vector] * 6
    return pl.pallas_call(
        widen_kernel,
        out_shape=[o[0] for o in outs],
        in_specs=[ANY] * 6 + [IN_VMEM],
        out_specs=[o[1] for o in outs],
        scratch_shapes=[
            pltpu.VMEM(f.shape, bf16),
            pltpu.VMEM(a.shape, bf16),
            pltpu.VMEM(q.shape, bf16),
            *[pltpu.VMEM(t.shape, t.dtype) for t in (lo, dual, gx)],
            pltpu.VMEM((6, width, width), f32),
            pltpu.SemaphoreType.DMA((15,)),
        ],
        compiler_params=pltpu.CompilerParams(vmem_limit_bytes=int(63.5 * 2**20)),
        cost_estimate=pl.CostEstimate(flops=0, bytes_accessed=19 << 20, transcendentals=0),
    )(lo, dual, gx, f, a, q, v)


def tuned_body(*args):
    (lo, dual, gx, gq, gk, gv, go, gwi, gwo, gg1, gs1, gbi, gbo, gg2, gs2) = widen(*tuned_layer(*sort_out(*args)))
    return lo, dual, gx, gq, gk, gv, go, gg1, gs1, gwi, gbi, gwo, gbo, gg2, gs2


def solution(mesh):
    tokens = P(("batch", "wide"), None)
    fits = mesh.shape["batch"] == 8 and mesh.shape["wide"] == 4
    return jax.shard_map(
        tuned_body if fits else plain_body,
        mesh=mesh,
        in_specs=(tokens, tokens, P(("batch", "wide")), P(), P(), P(), P(), P(), P(), P(None, "wide"), P("wide"),
                  P("wide", None), P(), P(), P(), tokens, tokens),
        out_specs=(tokens, tokens, tokens, P(), P(), P(), P(), P(), P(), P(None, "wide"), P("wide"),
                   P("wide", None), P(), P(), P()),
        check_vma=False,
    )
```

time: 428 us -> 129 us (0.30)
  waiting for transfers between devices: 252 us -> 0 us
  blocking collectives: 70.4 us -> 0 us
  Pallas kernels: 63.4 us -> 125 us
  local copies, waits for them, and re-layouts: 14.9 us -> 0 us
  between operations: 15.7 us -> 1.56 us
  other arithmetic: 8.74 us -> 0 us
    psum x2 -> x0, waiting for transfers between devices: 213 us -> none  [the longest x1 138 us: plain_body(): lax.psum((gw_o, gw_v, gw_qk, gvec), ('batch', 'wide'))]
    pallas_call x1 -> x2, Pallas kernels: 63.4 us -> 125 us  [the longest x1 116 us: tuned_layer(): pl.pallas_call(functools.partial(tuned_kernel, names), out_shape=list(out...]
    psum x2 -> x0, blocking collectives: 59 us -> none  [the longest x1 40.9 us: plain_body(): lax.psum((gw_o, gw_v, gw_qk, gvec), ('batch', 'wide'))]
    all_gather x2 -> x0, waiting for transfers between devices: 37.2 us -> none  [the longest x1 20 us: plain_body(): w_out_all = lax.all_gather(w_out, 'wide', axis=0, tiled=True)]
    all_gather x1 -> x0, blocking collectives: 5.96 us -> none  [plain_body(): bias_all = lax.all_gather(bias_in, 'wide', axis=0, tiled=True)]
    convert_element_type x4 -> x0, other arithmetic: 5.94 us -> none  [the longest x1 2.14 us: plain_body(): lax.psum(lax.psum_scatter(gwo2, 'wide', scatter_dimension=0, tiled=True),...]
    unnamed x1 -> x0, blocking collectives: 5.37 us -> none
    unnamed x27 -> x0, local copies, waits for them, and re-layouts: 4.99 us -> none
  transfers between devices with their start and end apart: 6 -> 0, of which waited for: 4 -> 0; matrix products, arithmetic and copies ran while one was open for 3% -> 0% of each run, Pallas kernels for 0% -> 0%
where the time goes in v2:
time: 129 us; the launch traced here: 127 us
  Pallas kernels  125 us (97%)
  between operations  1.56 us (1%)
    pallas_call x1, Pallas kernels, tuned_layer(): pl.pallas_call(functools.partial(tuned_kernel, names), out_shape=list(out...  116 us
    pallas_call x1, Pallas kernels, widen(): pl.pallas_call(widen_kernel, out_shape=[o[0] for o in outs], in_specs=[AN...  8.66 us

profile of v2, /device:TPU:1, one launch (start us, length us, event | category | flops | bytes accessed | tf_op | source)
XLA Modules:
  0.0 126.6 jit_solution(14451301640718953149)
XLA Ops:
  1.3 116.4 %shard_map.280 = (bf16[1024,512]{1,0:T(8,128)(2,1)}, f32[1024,512]{1,0:T(8,128)}, f32[1024,512]{1,0:T(8,128)}, bf16[2,512,512]{2,1,0:T(8,128)(2,1)}, bf16[2,512,...) custom-call(bf16[1024,512]{1,0:T(8,128)(2,1)} %refs_0_.1, bf16[512,512]{1,0:T(8,128)(2,1)} %refs_1_.1, ...), custom_call_target="tpu_custom_call" | custom-call | flops 24999999488 | bytes 31457280 | tf_op jit(solution)/shard_map/pallas_call | solution.py:1097
  117.7 8.7 %shard_map.281 = (bf16[1024,512]{1,0:T(8,128)(2,1)}, f32[1024,512]{1,0:T(8,128)}, f32[1024,512]{1,0:T(8,128)}, f32[512,512]{1,0:T(8,128)}, f32[512,512]{1,0:T(8,...) custom-call(bf16[1024,512]{1,0:T(8,128)(2,1)} %get-tuple-element.37., ...), custom_call_target="tpu_custom_call" | custom-call | bytes 19922944 | tf_op jit(solution)/shard_map/pallas_call | solution.py:1156

commit v3 on v2

--- a/solution.py
+++ b/solution.py
@@ -16,7 +16,21 @@
 PARTS = 4
 PRE_UNROLL = 1
 HALF_UNROLL = NORM_UNROLL = SECOND_UNROLL = FIRST_UNROLL = INPUT_UNROLL = 2
-Y_FIRST = (True, True, True, False, False, False)
+CORE, X, Y, NEXT, FAR, ZED, WIDE, BATCH = range(8)
+UNITS = (
+    (0, 0, 256, (Y, X, ZED)),
+    (0, 256, 256, (X, NEXT, FAR, Y)),
+    (1, 0, 256, (NEXT, Y, X, FAR)),
+    (1, 256, 256, (FAR, X, Y, NEXT)),
+)
+CHUNKS = (
+    (CORE, X, Y, ZED),
+    (CORE, X, Y, ZED),
+    (CORE, ZED, X, Y),
+    (CORE, Y, ZED, X),
+    (CORE, Y, X, ZED),
+    (WIDE, Y, ZED),
+)
 
 bf16 = jnp.bfloat16
 f32 = jnp.float32
@@ -427,9 +441,8 @@
 
 
 class Kind:
-    (W_X, W_Y, W_CORE, W_PASS, W_TURN, W_BIAS, F_AWAY, F_NEAR, F_X, F_Y, F_Y_OWN, F_NEXT, F_FAR,
-     G_FAR, G_Y, G_NEXT, A_CORE, A_ONE, A_TWO, A_NEXT, A_FAR, B_FAR, B_NEXT, B_TWO, B_ONE, B_CORE,
-     V_STEP) = range(27)
+    (W_X, W_Y, W_CORE, W_PASS, W_TURN, W_BIAS, F_CORE, F_AWAY, F_OWN, F_BACK, A_OUT, A_BACK,
+     V_STEP) = range(13)
 
 
 class Net:
@@ -448,6 +461,20 @@
         self.far = (((z + 2) % 4) * 2 + y, w)
         self.table = {}
         self.used = set()
+        def pair(peer, bit):
+            return bit, 2, [(peer, 1 - bit)]
+
+        self.axes = (
+            pair(self.core, c),
+            pair(self.ex, x),
+            pair(self.why, y),
+            pair(self.next, self.odd),
+            pair(self.far, self.high),
+            (z, 4, [(((z + k) % 4 * 2 + y, w), (z + k) % 4) for k in (1, 2, 3)]),
+            (w, 4, [(to, to[1]) for to in (self.core, self.ex, self.diagonal)]),
+            (b, 8, [(((b + k) % 8, w), (b + k) % 8) for k in range(1, 8)]),
+        )
+        self.units = []
         self.parts = []
         self.describe()
 
@@ -490,97 +517,120 @@
         else:
             pl.when(at == k)(functools.partial(self.tick, place, k))
 
+    def cut(self, base, size, mine, peers):
+        keep = lambda: self.span(base() + mine * size, size)
+        gives = [lambda at=at: self.span(base() + at * size, size) for _, at in peers]
+        return keep, gives, lambda: base() + mine * size
+
+    def group(self, act, *name):
+        k = 0
+        while (*name, k) in self.table:
+            act((*name, k))
+            k += 1
+        return k
+
     def span(self, start, size):
         return pl.ds(pl.multiple_of(start, size), size)
 
     def describe(self):
         r, copy, span = self.r, self.copy, self.span
-        y, x, c, odd, high = self.y, self.x, self.c, self.odd, self.high
         own = (r.wi_hbm, r.wo2_hbm)
         held = (r.wi, r.wo2)
         for m in range(2):
             copy((Kind.W_CORE, m), self.core, lambda m=m: own[m], lambda m=m: held[m].at[1])
-            for q in range(2):
-                mine = lambda q=q: span(y * 256 + q * 128, 128)
-                other = lambda q=q: span((1 - y) * 256 + q * 128, 128)
+            for q, (mine, other) in enumerate(self.slices(m)):
                 copy((Kind.W_X, m, q), self.ex, lambda m=m, f=mine: own[m].at[f()], lambda m=m, f=mine: held[m].at[2, f()])
-                copy((Kind.W_Y, m, q), self.why, lambda m=m, f=mine: held[m].at[2, f()], lambda m=m, f=mine: held[m].at[2, f()])
                 copy((Kind.W_PASS, m, q), self.core, lambda m=m, f=mine: held[m].at[2, f()], lambda m=m, f=mine: held[m].at[3, f()])
-                copy((Kind.W_TURN, m, q), self.core, lambda m=m, f=other: held[m].at[2, f()], lambda m=m, f=other: held[m].at[3, f()])
+                if other is not None:
+                    copy((Kind.W_Y, m, q), self.why, lambda m=m, f=mine: held[m].at[2, f()], lambda m=m, f=mine: held[m].at[2, f()])
+                    copy((Kind.W_TURN, m, q), self.core, lambda m=m, f=other: held[m].at[2, f()], lambda m=m, f=other: held[m].at[3, f()])
         for slot, to in ((1, self.core), (2, self.ex), (3, self.diagonal)):
             copy((Kind.W_BIAS, slot), to, lambda: r.bi.at[0], lambda slot=slot: r.bi.at[slot])
 
-        grads = (r.gwo2, r.gwi)
         for m in range(2):
-            copy((Kind.F_AWAY, m), self.core, lambda m=m: grads[m].at[3], lambda m=m: r.rca.at[m])
-            copy((Kind.F_NEAR, m), self.core, lambda m=m: grads[m].at[1], lambda m=m: r.rcd.at[m])
-            for h in range(2):
-                kept = lambda h=h: span(h * 256 + y * 128, 128)
-                away = lambda h=h: span(h * 256 + (1 - y) * 128, 128)
-                if h == 0:
-                    copy((Kind.F_X, m, h), self.ex, lambda m=m: grads[m].at[2, 0:256], lambda m=m: r.rx.at[m, 0:256])
+            for slot in (3, 1):
+                received = r.rca if slot == 3 else r.rcd
+                copy((Kind.F_CORE, m, slot), self.core, lambda m=m, s=slot: self.grad(m).at[s], lambda m=m, t=received: t.at[m])
+        for u, (m, start, size, order) in enumerate(UNITS):
+            grad, out = self.grad(m), r.fout.at[m]
+            base = lambda f=start: f
+            both, offset, levels, back = True, 0, [], []
+            for level, axis in enumerate(order):
+                mine, parts, peers = self.axes[axis]
+                if axis == X:
+                    both = False
+                    keep = lambda f=base, s=size: span(f(), s)
+                    gives = [keep]
                 else:
-                    copy((Kind.F_X, m, h), self.ex, lambda m=m, f=kept: grads[m].at[2, f()], lambda m=m: r.rx.at[m, 256:384])
-                    copy((Kind.F_Y_OWN, m, h), self.why, lambda m=m, f=away: grads[m].at[0, f()], lambda m=m: r.ry.at[m, 2])
-                slot = 0 if h == 0 else 2
-                copy((Kind.F_Y, m, h), self.why, lambda m=m, s=slot, f=away: grads[m].at[s, f()], lambda m=m, h=h: r.ry.at[m, h])
-                u = m * 2 + h
-                near = lambda h=h: span(h * 256 + y * 128 + odd * 64, 64)
-                near_y = lambda h=h: span(h * 256 + (1 - y) * 128 + odd * 64, 64)
-                gone = lambda h=h: span(h * 256 + y * 128 + (1 - odd) * 64, 64)
-                piece = lambda h=h: span(h * 256 + y * 128 + odd * 64 + high * 32, 32)
-                gone2 = lambda h=h: span(h * 256 + y * 128 + odd * 64 + (1 - high) * 32, 32)
-                copy((Kind.F_NEXT, m, h), self.next, lambda m=m, f=gone: grads[m].at[0, f()], lambda u=u: r.rn.at[u])
-                copy((Kind.F_FAR, m, h), self.far, lambda m=m, f=gone2: grads[m].at[0, f()], lambda u=u: r.rf.at[u])
-                for kind, to, rows in ((Kind.G_FAR, self.far, piece), (Kind.G_Y, self.why, near)):
-                    copy((kind, m, h), to, lambda m=m, f=rows: r.fout.at[m, f()], lambda m=m, f=rows: r.fout.at[m, f()])
-                for k, rows in enumerate((near, near_y)):
-                    copy((Kind.G_NEXT, m, h, k), self.next, lambda m=m, f=rows: r.fout.at[m, f()], lambda m=m, f=rows: r.fout.at[m, f()])
+                    size //= parts
+                    keep, gives, base = self.cut(base, size, mine, peers)
+                    back.append((axis, keep))
+                landing = [[], []]
+                for k, (to, _) in enumerate(peers):
+                    for slot, kind, wanted in ((2, Kind.F_AWAY, both or axis == X), (0, Kind.F_OWN, axis != X)):
+                        if wanted:
+                            target = r.rf.at[u, offset : offset + size]
+                            offset += size
+                            landing[slot // 2].append(target)
+                            copy((kind, u, level, k), to, lambda g=grad, s=slot, f=gives[k]: g.at[s, f()], lambda t=target: t)
+                levels.append((axis, keep, landing))
+            for step, (axis, keep) in enumerate(reversed(back)):
+                for k, (to, _) in enumerate(self.axes[axis][2]):
+                    copy((Kind.F_BACK, u, step, k), to, lambda o=out, f=keep: o.at[f()], lambda o=out, f=keep: o.at[f()])
+            self.units.append((m, levels))
 
         for n in range(2 + PARTS):
-            refs = (r.gw, r.ac, r.a1, r.a2, r.a3, r.a4, r.aout)
-            at = n
-            if n >= 2:
-                refs = (r.gqk, r.qc, r.q1, r.q2, r.q3, r.q4, r.qout)
-                at = n - 2
-            grad, *received, out = [ref.at[at] for ref in refs]
-            first, second = ((self.ex, x), (self.why, y))
-            if Y_FIRST[n]:
-                first, second = second, first
-            levels = ((self.core, c), first, second, (self.next, odd), (self.far, high))
-            kinds = (Kind.A_CORE, Kind.A_ONE, Kind.A_TWO, Kind.A_NEXT, Kind.A_FAR)
-            back = (Kind.B_CORE, Kind.B_ONE, Kind.B_TWO, Kind.B_NEXT, Kind.B_FAR)
+            if n < 2:
+                grad, received, out = r.gw.at[n], r.ra.at[n], r.aout.at[n]
+            else:
+                grad, received, out = r.gqk.at[n - 2], r.rq.at[n - 2], r.qout.at[n - 2]
             size = grad.shape[0]
             base = lambda: 0
-            keeps = []
-            for level, (to, bit) in enumerate(levels):
-                size //= 2
-                keep = lambda f=base, p=bit, s=size: span(f() + p * s, s)
-                give = lambda f=base, p=bit, s=size: span(f() + (1 - p) * s, s)
-                base = lambda f=base, p=bit, s=size: f() + p * s
-                keeps.append(keep)
-                copy((kinds[level], n), to, lambda g=grad, f=give: g.at[f()], lambda t=received[level]: t)
-                copy((back[level], n), to, lambda o=out, f=keep: o.at[f()], lambda o=out, f=keep: o.at[f()])
-            self.parts.append((grad, received, out, keeps))
+            offset, levels = 0, []
+            for level, axis in enumerate(CHUNKS[n]):
+                mine, parts, peers = self.axes[axis]
+                size //= parts
+                keep, gives, base = self.cut(base, size, mine, peers)
+                landing = []
+                for k, (to, _) in enumerate(peers):
+                    target = received.at[offset : offset + size]
+                    offset += size
+                    landing.append(target)
+                    copy((Kind.A_OUT, n, level, k), to, lambda g=grad, f=gives[k]: g.at[f()], lambda t=target: t)
+                    copy((Kind.A_BACK, n, level, k), to, lambda o=out, f=keep: o.at[f()], lambda o=out, f=keep: o.at[f()])
+                levels.append((keep, landing))
+            self.parts.append((grad, out, levels))
 
         for at, to in enumerate((self.core, self.ex, self.why, self.next, self.far)):
             copy((Kind.V_STEP, at), to, lambda at=at: r.vs.at[at], lambda at=at: r.vr.at[at])
 
     def enter(self):
         barrier = pltpu.get_barrier_semaphore()
-        peers = [self.core, self.ex, self.diagonal, self.why, self.next, self.far]
+        peers = [to for axis in (WIDE, BATCH) for to, _ in self.axes[axis][2]]
         for peer in peers:
             pl.semaphore_signal(barrier, inc=1, device_id=peer, device_id_type=pl.DeviceIdType.MESH)
         pl.semaphore_wait(barrier, len(peers))
         for slot in (1, 2, 3):
             self.start((Kind.W_BIAS, slot))
         for m in range(2):
-            self.start((Kind.W_X, m, 0), (Kind.W_X, m, 1))
+            self.group(self.start, Kind.W_X, m)
         self.start((Kind.W_CORE, 0), (Kind.W_CORE, 1))
+
+    def slices(self, m):
+        y = self.y
+        if m == 0:
+            for q in range(4):
+                yield (lambda q=q: self.span(y * 256 + q * 64, 64)), (lambda q=q: self.span((1 - y) * 256 + q * 64, 64))
+        else:
+            yield (lambda: self.span(y * 256, 128)), (lambda: self.span((1 - y) * 256, 128))
+            for row in (128, 384):
+                yield (lambda row=row: self.span(row, 128)), None
 
     def pass_x(self, m, q):
         self.got((Kind.W_X, m, q))
-        self.start((Kind.W_Y, m, q), (Kind.W_PASS, m, q))
+        if (Kind.W_Y, m, q) in self.table:
+            self.start((Kind.W_Y, m, q))
+        self.start((Kind.W_PASS, m, q))
 
     def pass_y(self, m, q):
         self.got((Kind.W_Y, m, q))
@@ -592,132 +642,87 @@
         self.got((Kind.W_CORE, m))
 
     def arrived_far(self, m):
-        for q in range(2):
-            self.got((Kind.W_PASS, m, q), (Kind.W_TURN, m, q))
+        self.group(self.got, Kind.W_PASS, m)
+        self.group(self.got, Kind.W_TURN, m)
 
     def grad(self, m):
         return (self.r.gwo2, self.r.gwi)[m]
 
     def f_core(self, m, slot):
-        self.start((Kind.F_AWAY if slot == 3 else Kind.F_NEAR, m))
+        self.start((Kind.F_CORE, m, slot))
+
+    def f_begin(self, kind, m):
+        for u, unit in enumerate(self.units):
+            if unit[0] == m:
+                self.group(self.start, kind, u, 0)
 
     def f_x(self, m):
-        r, grad = self.r, self.grad(m)
-        self.got((Kind.F_AWAY, m))
-        grad[2] = (grad[2].astype(f32) + r.rca[m].astype(f32)).astype(bf16)
-        self.start((Kind.F_X, m, 0), (Kind.F_Y, m, 1))
+        self.got((Kind.F_CORE, m, 3))
+        grad = self.grad(m)
+        grad[2] = grad[2] + self.r.rca[m]
+        self.f_begin(Kind.F_AWAY, m)
 
     def f_near(self, m):
-        r, grad = self.r, self.grad(m)
-        self.got((Kind.F_NEAR, m))
-        grad[0] = (grad[0].astype(f32) + r.rcd[m].astype(f32)).astype(bf16)
-        self.start((Kind.F_Y_OWN, m, 1))
-
-    def f_own(self, m, h):
-        r, grad = self.r, self.grad(m)
-        y = self.y
-        if h == 0:
-            self.got((Kind.F_X, m, 0))
-            total = grad[0, 0:256].astype(f32) + r.rx[m, 0:256].astype(f32)
-            grad[0, 0:256] = total.astype(bf16)
-            self.start((Kind.F_Y, m, 0))
+        self.got((Kind.F_CORE, m, 1))
+        grad = self.grad(m)
+        grad[0] = grad[0] + self.r.rcd[m]
+        self.f_begin(Kind.F_OWN, m)
+
+    def plus(self, total, landing):
+        if len(landing) == 1:
+            return total + landing[0][...]
+        total = total.astype(f32)
+        for part in landing:
+            total += part[...].astype(f32)
+        return total.astype(bf16)
+
+    def f_step(self, u, level):
+        m, levels = self.units[u]
+        grad = self.grad(m)
+        axis, keep, (landing_own, landing_away) = levels[level]
+        s = keep()
+        if landing_away:
+            self.group(self.got, Kind.F_AWAY, u, level)
+            if axis != X:
+                grad[2, s] = self.plus(grad[2, s], landing_away)
+        if landing_own:
+            self.group(self.got, Kind.F_OWN, u, level)
+        total = self.plus(grad[0, s], landing_away if axis == X else landing_own)
+        if level == len(levels) - 1:
+            self.r.fout[m, s] = total
+            self.group(self.start, Kind.F_BACK, u, 0)
         else:
-            self.got((Kind.F_Y, m, 1))
-            s = self.span(256 + y * 128, 128)
-            grad[2, s] = (grad[2, s].astype(f32) + r.ry[m, 1].astype(f32)).astype(bf16)
-            self.start((Kind.F_X, m, 1))
-
-    def f_y(self, m, h):
-        r, grad = self.r, self.grad(m)
-        s = self.span(h * 256 + self.y * 128, 128)
-        if h == 0:
-            self.got((Kind.F_Y, m, 0))
-            total = grad[0, s].astype(f32) + r.ry[m, 0].astype(f32)
+            grad[0, s] = total
+            self.group(self.start, Kind.F_AWAY, u, level + 1)
+            self.group(self.start, Kind.F_OWN, u, level + 1)
+
+    def f_back(self, u, step):
+        self.group(self.got, Kind.F_BACK, u, step)
+        if not self.group(self.start, Kind.F_BACK, u, step + 1):
+            self.r.put("f", u)
+
+    def a_core(self, n):
+        self.group(self.start, Kind.A_OUT, n, 0)
+
+    def a_step(self, n, level):
+        grad, out, levels = self.parts[n]
+        self.group(self.got, Kind.A_OUT, n, level)
+        keep, landing = levels[level]
+        s = keep()
+        total = self.plus(grad[s], landing)
+        if level + 1 < len(levels):
+            grad[s] = total
+            self.group(self.start, Kind.A_OUT, n, level + 1)
         else:
-            self.got((Kind.F_Y_OWN, m, 1), (Kind.F_X, m, 1))
-            total = grad[0, s].astype(f32) + r.ry[m, 2].astype(f32) + r.rx[m, 256:384].astype(f32)
-        grad[0, s] = total.astype(bf16)
-        self.start((Kind.F_NEXT, m, h))
-
-    def f_z(self, m, h):
-        r, grad = self.r, self.grad(m)
-        self.got((Kind.F_NEXT, m, h))
-        s = self.span(h * 256 + self.y * 128 + self.odd * 64, 64)
-        grad[0, s] = (grad[0, s].astype(f32) + r.rn[m * 2 + h].astype(f32)).astype(bf16)
-        self.start((Kind.F_FAR, m, h))
-
-    def f_zz(self, m, h):
-        r, grad = self.r, self.grad(m)
-        self.got((Kind.F_FAR, m, h))
-        s = self.span(h * 256 + self.y * 128 + self.odd * 64 + self.high * 32, 32)
-        r.fout[m, s] = (grad[0, s].astype(f32) + r.rf[m * 2 + h].astype(f32)).astype(bf16)
-        self.start((Kind.G_FAR, m, h))
-
-    def f_g(self, m, h):
-        self.got((Kind.G_FAR, m, h))
-        self.start((Kind.G_Y, m, h), (Kind.G_NEXT, m, h, 0))
-
-    def f_gg(self, m, h):
-        self.got((Kind.G_Y, m, h))
-        self.start((Kind.G_NEXT, m, h, 1))
-
-    def f_end(self, m, h):
-        self.got((Kind.G_NEXT, m, h, 0), (Kind.G_NEXT, m, h, 1))
-        self.r.put("f", m * 2 + h)
-
-    def a_core(self, n):
-        self.start((Kind.A_CORE, n))
-
-    def a_sum(self, n, level, target=None):
-        grad, received, _, keeps = self.parts[n]
-        s = keeps[level]()
-        total = grad[s].astype(f32) + received[level][...].astype(f32)
-        (grad if target is None else target)[s] = total.astype(bf16)
-
-    def a_1(self, n):
-        self.got((Kind.A_CORE, n))
-        self.a_sum(n, 0)
-        self.start((Kind.A_ONE, n))
-
-    def a_2(self, n):
-        self.got((Kind.A_ONE, n))
-        self.a_sum(n, 1)
-        self.start((Kind.A_TWO, n))
-
-    def a_z(self, n):
-        self.got((Kind.A_TWO, n))
-        self.a_sum(n, 2)
-        self.start((Kind.A_NEXT, n))
-
-    def a_zz(self, n):
-        self.got((Kind.A_NEXT, n))
-        self.a_sum(n, 3)
-        self.start((Kind.A_FAR, n))
-
-    def a_g(self, n):
-        self.got((Kind.A_FAR, n))
-        self.a_sum(n, 4, self.parts[n][2])
-        self.start((Kind.B_FAR, n))
-
-    def a_gg(self, n):
-        self.got((Kind.B_FAR, n))
-        self.start((Kind.B_NEXT, n))
-
-    def a_3(self, n):
-        self.got((Kind.B_NEXT, n))
-        self.start((Kind.B_TWO, n))
-
-    def a_4(self, n):
-        self.got((Kind.B_TWO, n))
-        self.start((Kind.B_ONE, n))
-
-    def a_5(self, n):
-        self.got((Kind.B_ONE, n))
-        self.start((Kind.B_CORE, n))
-
-    def a_end(self, n):
-        self.got((Kind.B_CORE, n))
-        self.r.put("a", n)
+            out[s] = total
+            self.group(self.start, Kind.A_BACK, n, level)
+
+    def a_back(self, n, level):
+        self.group(self.got, Kind.A_BACK, n, level)
+        if level:
+            self.group(self.start, Kind.A_BACK, n, level - 1)
+        else:
+            self.r.put("a", n)
 
     def v_core(self):
         r = self.r
@@ -837,198 +842,194 @@
     plan[(At.ATTEND, 0)] = (
         (n.pass_x, 0, 0),
     )
+    plan[(At.ATTEND, 3)] = (
+        (n.pass_x, 0, 1),
+    )
     plan[(At.ATTEND, 5)] = (
-        (n.pass_x, 0, 1),
+        (n.pass_x, 0, 2),
+    )
+    plan[(At.ATTEND, 7)] = (
+        (n.pass_x, 0, 3),
     )
     plan[(At.ATTEND, 8)] = (
         (n.pass_y, 0, 0),
     )
     plan[(At.HIDDEN,)] = (
+        (n.pass_y, 0, 1),
         (n.pass_x, 1, 0),
         (n.arrived_near, 0),
     )
     plan[(At.HALVES, 3)] = (
-        (n.pass_y, 0, 1),
+        (n.pass_y, 0, 2),
+    )
+    plan[(At.OTHERS,)] = (
+        (n.pass_y, 0, 3),
         (n.pass_x, 1, 1),
-    )
-    plan[(At.OTHERS,)] = (
+        (n.pass_x, 1, 2),
+        (n.arrived_far, 0),
+    )
+    plan[(At.HALVES2, 1)] = (
         (n.pass_y, 1, 0),
-        (n.arrived_far, 0),
+    )
+    plan[(At.OUT, 3)] = (
+        (n.f_core, 0, 3),
+    )
+    plan[(At.OUT, 1)] = (
+        (n.f_core, 0, 1),
+    )
+    plan[(At.PRE, 2)] = (
+        (n.f_x, 0),
+    )
+    plan[(At.PRE, 3)] = (
+        (n.f_near, 0),
+    )
+    plan[(At.IN, 3)] = (
+        (n.f_core, 1, 3),
+    )
+    plan[(At.IN, 1)] = (
+        (n.f_core, 1, 1),
+    )
+    plan[(At.FIRST, 1)] = (
+        (n.f_x, 1),
+    )
+    plan[(At.FIRST, 3)] = (
+        (n.f_near, 1),
+    )
+    plan[(At.W_OUTPUT,)] = (
+        (n.a_core, 0),
+        (n.f_step, 1, 0),
+        (n.v_core,),
+        (n.f_step, 0, 0),
+    )
+    plan[(At.VALUES, 6)] = (
+        (n.a_step, 0, 0),
+        (n.v_next, 0),
+    )
+    plan[(At.W_VALUE,)] = (
+        (n.a_core, 1),
+    )
+    plan[(At.SCORES, 1)] = (
+        (n.f_step, 0, 1),
+    )
+    plan[(At.SCORES, 2)] = (
+        (n.a_core, 2),
+        (n.a_step, 1, 0),
+        (n.f_step, 2, 0),
+    )
+    plan[(At.SCORES, 3)] = (
+        (n.a_step, 0, 1),
+    )
+    plan[(At.SCORES, 4)] = (
+        (n.a_core, 3),
+        (n.a_step, 2, 0),
+        (n.v_next, 1),
+    )
+    plan[(At.SCORES, 5)] = (
+        (n.f_step, 3, 0),
+    )
+    plan[(At.SCORES, 6)] = (
+        (n.f_step, 1, 1),
+        (n.a_step, 3, 0),
+        (n.a_core, 4),
+        (n.a_step, 1, 1),
+        (n.f_step, 2, 1),
+    )
+    plan[(At.SCORES, 7)] = (
+        (n.a_step, 0, 2),
+    )
+    plan[(At.SCORES, 8)] = (
+        (n.a_core, 5),
+        (n.a_step, 4, 0),
+        (n.f_step, 0, 2),
+        (n.v_next, 2),
+    )
+    plan[(At.INPUT, 1)] = (
+        (n.a_step, 2, 1),
+        (n.a_step, 3, 1),
+        (n.f_step, 3, 1),
+    )
+    plan[(At.INPUT, 3)] = (
+        (n.a_step, 1, 2),
+        (n.f_step, 1, 2),
+        (n.f_step, 2, 2),
+    )
+    plan[(At.END,)] = (
+        (n.a_step, 4, 1),
+        (n.a_step, 0, 3),
+        (n.a_step, 5, 0),
+        (n.v_next, 3),
+        (n.a_step, 2, 2),
+        (n.f_step, 3, 2),
+        (n.f_step, 1, 3),
+        (n.f_back, 0, 0),
+        (n.a_step, 4, 2),
+        (n.a_step, 3, 2),
+        (n.a_step, 5, 1),
+        (n.a_step, 1, 3),
+        (n.a_step, 2, 3),
+        (n.f_step, 2, 3),
+        (n.f_step, 3, 3),
+        (n.f_back, 1, 0),
+        (n.a_step, 3, 3),
+        (n.a_back, 0, 3),
+        (n.v_next, 4),
+        (n.f_back, 0, 1),
+        (n.a_back, 2, 3),
+        (n.a_step, 4, 3),
+        (n.a_step, 5, 2),
+        (n.a_back, 3, 3),
+        (n.f_back, 3, 0),
+        (n.a_back, 1, 3),
+        (n.f_back, 2, 0),
+        (n.a_back, 0, 2),
+        (n.a_back, 2, 2),
+        (n.f_back, 1, 1),
+        (n.f_back, 3, 1),
+        (n.a_back, 4, 3),
+        (n.a_back, 5, 2),
+        (n.a_back, 1, 2),
+        (n.a_back, 3, 2),
+        (n.f_back, 2, 1),
+        (n.a_back, 0, 1),
+        (n.a_back, 4, 2),
+        (n.a_back, 2, 1),
+        (n.a_back, 5, 1),
+        (n.f_back, 1, 2),
+        (n.a_back, 0, 0),
+        (n.a_back, 3, 1),
+        (n.a_back, 1, 1),
+        (n.a_back, 2, 0),
+        (n.a_back, 4, 1),
+        (n.f_back, 3, 2),
+        (n.a_back, 3, 0),
+        (n.f_back, 2, 2),
+        (n.a_back, 1, 0),
+        (n.a_back, 5, 0),
+        (n.a_back, 4, 0),
     )
     plan[(At.BRANCH,)] = (
-        (n.pass_y, 1, 1),
         (n.arrived_near, 1),
         (n.arrived_far, 1),
     )
-    plan[(At.OUT, 3)] = (
-        (n.f_core, 0, 3),
-    )
-    plan[(At.OUT, 1)] = (
-        (n.f_core, 0, 1),
-    )
-    plan[(At.PRE, 1)] = (
-        (n.f_x, 0),
-        (n.f_near, 0),
-    )
-    plan[(At.IN, 3)] = (
-        (n.f_core, 1, 3),
-    )
-    plan[(At.IN, 1)] = (
-        (n.f_core, 1, 1),
-    )
-    plan[(At.FIRST, 1)] = (
-        (n.f_x, 1),
-        (n.f_own, 0, 1),
-        (n.f_near, 1),
-        (n.f_own, 0, 0),
-    )
-    plan[(At.W_OUTPUT,)] = (
-        (n.a_core, 0),
-        (n.v_core,),
-    )
-    plan[(At.VALUES, 1)] = (
-        (n.f_own, 1, 1),
-    )
-    plan[(At.VALUES, 4)] = (
-        (n.v_next, 0),
-        (n.a_1, 0),
-    )
-    plan[(At.W_VALUE,)] = (
-        (n.a_core, 1),
-        (n.f_own, 1, 0),
-    )
-    plan[(At.SCORES, 1)] = (
-        (n.a_1, 1),
-        (n.f_y, 0, 0),
-        (n.f_y, 0, 1),
-    )
-    plan[(At.SCORES, 2)] = (
-        (n.a_core, 2),
-    )
-    plan[(At.SCORES, 3)] = (
-        (n.a_2, 0),
-        (n.f_y, 1, 1),
-        (n.v_next, 1),
-        (n.a_1, 2),
-    )
-    plan[(At.SCORES, 4)] = (
-        (n.a_core, 3),
-        (n.f_z, 0, 0),
-    )
-    plan[(At.SCORES, 5)] = (
-        (n.f_z, 0, 1),
-        (n.f_y, 1, 0),
-        (n.a_z, 0),
-        (n.a_1, 3),
-        (n.f_z, 1, 1),
-    )
-    plan[(At.SCORES, 6)] = (
-        (n.a_core, 4),
-        (n.a_2, 1),
-    )
-    plan[(At.SCORES, 7)] = (
-        (n.f_zz, 0, 0),
-        (n.v_next, 2),
-    )
-    plan[(At.SCORES, 8)] = (
-        (n.a_core, 5),
-        (n.a_1, 4),
-        (n.a_2, 3),
-        (n.a_2, 2),
-        (n.a_zz, 0),
-        (n.f_zz, 0, 1),
-        (n.a_z, 1),
-        (n.f_z, 1, 0),
-    )
-    plan[(At.INPUT, 1)] = (
-        (n.f_zz, 1, 1),
-        (n.v_next, 3),
-        (n.a_1, 5),
-    )
-    plan[(At.INPUT, 3)] = (
-        (n.a_2, 4),
-        (n.a_z, 3),
-        (n.a_g, 0),
-        (n.a_z, 2),
-        (n.a_zz, 1),
-        (n.f_g, 0, 0),
-    )
-    plan[(At.END,)] = (
-        (n.f_g, 0, 1),
-        (n.a_2, 5),
-        (n.a_z, 4),
-        (n.a_zz, 3),
-        (n.f_zz, 1, 0),
-        (n.a_zz, 2),
-        (n.f_gg, 0, 0),
-        (n.f_g, 1, 1),
-        (n.f_gg, 0, 1),
-        (n.v_next, 4),
-        (n.a_z, 5),
-        (n.a_gg, 0),
-        (n.a_zz, 4),
-        (n.a_g, 1),
-        (n.a_g, 3),
-        (n.f_gg, 1, 1),
-        (n.f_g, 1, 0),
-        (n.a_g, 2),
-        (n.f_end, 0, 0),
-        (n.a_g, 4),
-        (n.a_gg, 1),
-        (n.a_gg, 3),
-        (n.f_gg, 1, 0),
-        (n.a_gg, 2),
-        (n.f_end, 0, 1),
-        (n.a_zz, 5),
-        (n.a_gg, 4),
-        (n.a_3, 0),
-        (n.f_end, 1, 1),
-        (n.a_g, 5),
-        (n.a_4, 0),
-        (n.a_3, 1),
-        (n.a_3, 3),
-        (n.a_gg, 5),
-        (n.f_end, 1, 0),
-        (n.a_3, 2),
-        (n.a_3, 4),
-        (n.a_3, 5),
-        (n.a_4, 1),
-        (n.a_5, 0),
-        (n.a_4, 3),
-        (n.a_4, 2),
-        (n.a_4, 4),
-        (n.a_end, 0),
-        (n.a_4, 5),
-        (n.a_5, 3),
-        (n.a_5, 1),
-        (n.a_5, 4),
-        (n.a_end, 3),
-        (n.a_5, 2),
-        (n.a_5, 5),
-        (n.a_end, 1),
-        (n.a_end, 4),
-        (n.a_end, 2),
-        (n.a_end, 5),
-    )
     return plan
 
 
-COPIES = 144
+COPIES = 224
 
 
 def tuned_kernel(names, *refs):
     r = Refs(names, refs)
     base = begin(r, r.x.shape[0])
     sems = r.sems
-    for u in range(4):
-        m, cut = u // 2, slice(u % 2 * 256, u % 2 * 256 + 256)
+    for u, (m, start, size, _) in enumerate(UNITS):
+        cut = slice(start, start + size)
         r.outs["f", u] = (r.fout.at[m, cut], r.f_out.at[m, cut], sems.at[base + u])
     for n in range(2 + PARTS):
         pair = (r.aout.at[n], r.a_out.at[n]) if n < 2 else (r.qout.at[n - 2], r.q_out.at[n - 2])
-        r.outs["a", n] = (*pair, sems.at[base + 4 + n])
-    r.outs["v", 0] = (r.vs.at[5], r.v_out, sems.at[base + 6 + PARTS])
-    r.fetch("wi", r.wi_hbm, r.wi.at[0], sems.at[base + 7 + PARTS])
-    r.fetch("wo2", r.wo2_hbm, r.wo2.at[0], sems.at[base + 8 + PARTS])
+        r.outs["a", n] = (*pair, sems.at[base + len(UNITS) + n])
+    r.outs["v", 0] = (r.vs.at[5], r.v_out, sems.at[base + len(UNITS) + 2 + PARTS])
+    r.fetch("wi", r.wi_hbm, r.wi.at[0], sems.at[base + len(UNITS) + 3 + PARTS])
+    r.fetch("wo2", r.wo2_hbm, r.wo2.at[0], sems.at[base + len(UNITS) + 4 + PARTS])
     r.bi[0] = jnp.broadcast_to(r.bias_in[...].astype(f32)[None], r.bi.shape[1:])
     net = Net(r, steps())
     net.enter()
@@ -1070,26 +1071,15 @@
         gbi=vmem((hidden, 1, HALF), f32),
         rca=vmem((2, HALF, width), bf16),
         rcd=vmem((2, HALF, width), bf16),
-        rx=vmem((2, 384, width), bf16),
-        ry=vmem((2, 3, 128, width), bf16),
-        rn=vmem((4, 64, width), bf16),
-        rf=vmem((4, 32, width), bf16),
+        rf=vmem((len(UNITS), max(unit[2] for unit in UNITS) * 15 // 8, width), bf16),
         fout=vmem((2, HALF, width), bf16),
-        ac=vmem((2, 256, width), bf16),
-        a1=vmem((2, 128, width), bf16),
-        a2=vmem((2, 64, width), bf16),
-        a3=vmem((2, 32, width), bf16),
-        a4=vmem((2, 16, width), bf16),
+        ra=vmem((2, width * 31 // 32, width), bf16),
         aout=vmem((2, width, width), bf16),
-        qc=vmem((PARTS, 256, part), bf16),
-        q1=vmem((PARTS, 128, part), bf16),
-        q2=vmem((PARTS, 64, part), bf16),
-        q3=vmem((PARTS, 32, part), bf16),
-        q4=vmem((PARTS, 16, part), bf16),
+        rq=vmem((PARTS, width * 31 // 32, part), bf16),
         qout=vmem((PARTS, width, part), bf16),
         vs=vmem((6, 16, width), f32),
         vr=vmem((5, 16, width), f32),
-        sems=pltpu.SemaphoreType.DMA((len(FETCHED) + 4 + 9 + PARTS,)),
+        sems=pltpu.SemaphoreType.DMA((len(FETCHED) + 4 + len(UNITS) + 5 + PARTS,)),
         send_sem=pltpu.SemaphoreType.DMA((COPIES,)),
         recv_sem=pltpu.SemaphoreType.DMA((COPIES,)),
     )
@@ -1109,42 +1099,48 @@
 
 def widen_kernel(lo, dual, gx, f, a, q, v, lo_out, dual_out, gx_out, gq, gk, gv, go, gwi, gwo,
                  gg1, gs1, gbi, gbo, gg2, gs2, f_low, a_low, q_low, lo_held, dual_held, gx_held, wide, sems):
-    loads = ((f, f_low), (a, a_low), (q, q_low), (dual, dual_held), (gx, gx_held), (lo, lo_held))
-    copies = []
-    for at, (source, target) in enumerate(loads):
-        copies.append(pltpu.make_async_copy(source, target, sems.at[at]))
-        copies[at].start()
+    def copy(source, target, at):
+        made = pltpu.make_async_copy(source, target, sems.at[at])
+        made.start()
+        return made
+
+    low = [copy(*pair, at) for at, pair in enumerate(((f, f_low), (a, a_low), (q, q_low)))]
+    moves = []
+    for source, held, target in ((dual, dual_held, dual_out), (gx, gx_held, gx_out), (lo, lo_held, lo_out)):
+        for at in range(source.shape[0] // BLOCK):
+            rows = rows_of(at)
+            moves.append((source.at[rows], held.at[rows], target.at[rows]))
+    loads = [copy(source, held, 3 + at) for at, (source, held, _) in enumerate(moves)]
+    stores = []
+
+    def store(source, target):
+        stores.append(copy(source, target, 3 + len(moves) + len(stores)))
+
+    def widened(at, value, target):
+        wide[at] = value.astype(f32)
+        store(wide.at[at], target)
+
     for at, out in enumerate((gg1, gs1, gbo, gg2, gs2)):
         out[...] = v[at]
     gbi[...] = v[12]
-    outs = []
-
-    def send(source, target):
-        copy = pltpu.make_async_copy(source, target, sems.at[6 + len(outs)])
-        copy.start()
-        outs.append(copy)
-
-    copies[0].wait()
-    wide[0] = f_low[0].astype(f32)
-    send(wide.at[0], gwo)
-    wide[1] = f_low[1].astype(f32)
-    send(wide.at[1], gwi)
-    copies[1].wait()
-    wide[2] = a_low[0].astype(f32)
-    send(wide.at[2], go)
-    wide[3] = a_low[1].astype(f32)
-    send(wide.at[3], gv)
-    copies[2].wait()
+    low[0].wait()
+    widened(0, f_low[0], gwo)
+    widened(1, f_low[1], gwi)
+    low[1].wait()
+    widened(2, a_low[0], go)
+    widened(3, a_low[1], gv)
+    low[2].wait()
     part = q.shape[2] // 2
     for at, target in ((4, gq), (5, gk)):
+        cols = span_of(at - 4, part)
         for p in range(PARTS):
-            wide[at, :, p * part : (p + 1) * part] = q_low[p, :, (at - 4) * part : (at - 3) * part].astype(f32)
-        send(wide.at[at], target)
-    for at, source, target in ((3, dual_held, dual_out), (4, gx_held, gx_out), (5, lo_held, lo_out)):
-        copies[at].wait()
-        send(source, target)
-    for copy in outs:
-        copy.wait()
+            wide[at, :, p * part : (p + 1) * part] = q_low[p, :, cols].astype(f32)
+        store(wide.at[at], target)
+    for load, (_, held, target) in zip(loads, moves):
+        load.wait()
+        store(held, target)
+    for made in stores:
+        made.wait()
 
 
 def widen(lo, dual, gx, f, a, q, v):
@@ -1164,7 +1160,7 @@
             pltpu.VMEM(q.shape, bf16),
             *[pltpu.VMEM(t.shape, t.dtype) for t in (lo, dual, gx)],
             pltpu.VMEM((6, width, width), f32),
-            pltpu.SemaphoreType.DMA((15,)),
+            pltpu.SemaphoreType.DMA((9 + 6 * (lo.shape[0] // BLOCK),)),
         ],
         compiler_params=pltpu.CompilerParams(vmem_limit_bytes=int(63.5 * 2**20)),
         cost_estimate=pl.CostEstimate(flops=0, bytes_accessed=19 << 20, transcendentals=0),

time: 129 us -> 111 us (0.86); the launches traced: 127 us -> 111 us
  Pallas kernels: 125 us -> 109 us
    pallas_call x1, Pallas kernels: 116 us -> 101 us  [tuned_layer(): pl.pallas_call(functools.partial(tuned_kernel, names), out_shape=list(out...]
where the time goes in v3:
time: 111 us
  Pallas kernels  109 us (98%)
  between operations  1.51 us (1%)
    pallas_call x1, Pallas kernels, tuned_layer(): pl.pallas_call(functools.partial(tuned_kernel, names), out_shape=list(out...  101 us
    pallas_call x1, Pallas kernels, widen(): pl.pallas_call(widen_kernel, out_shape=[o[0] for o in outs], in_specs=[AN...  8.53 us

profile of v3, /device:TPU:1, one launch (start us, length us, event | category | flops | bytes accessed | tf_op | source)
XLA Modules:
  0.0 110.6 jit_solution(15150921560754558352)
XLA Ops:
  1.3 100.5 %shard_map.280 = (bf16[1024,512]{1,0:T(8,128)(2,1)}, f32[1024,512]{1,0:T(8,128)}, f32[1024,512]{1,0:T(8,128)}, bf16[2,512,512]{2,1,0:T(8,128)(2,1)}, bf16[2,512,...) custom-call(bf16[1024,512]{1,0:T(8,128)(2,1)} %refs_0_.1, bf16[512,512]{1,0:T(8,128)(2,1)} %refs_1_.1, ...), custom_call_target="tpu_custom_call" | custom-call | flops 24999999488 | bytes 31457280 | tf_op jit(solution)/shard_map/pallas_call | solution.py:1087
  101.8 8.5 %shard_map.281 = (bf16[1024,512]{1,0:T(8,128)(2,1)}, f32[1024,512]{1,0:T(8,128)}, f32[1024,512]{1,0:T(8,128)}, f32[512,512]{1,0:T(8,128)}, f32[512,512]{1,0:T(8,...) custom-call(bf16[1024,512]{1,0:T(8,128)(2,1)} %get-tuple-element.37., ...), custom_call_target="tpu_custom_call" | custom-call | bytes 19922944 | tf_op jit(solution)/shard_map/pallas_call | solution.py:1152

commit v4 on v3

--- a/solution.py
+++ b/solution.py
@@ -18,16 +18,16 @@
 HALF_UNROLL = NORM_UNROLL = SECOND_UNROLL = FIRST_UNROLL = INPUT_UNROLL = 2
 CORE, X, Y, NEXT, FAR, ZED, WIDE, BATCH = range(8)
 UNITS = (
-    (0, 0, 256, (Y, X, ZED)),
-    (0, 256, 256, (X, NEXT, FAR, Y)),
-    (1, 0, 256, (NEXT, Y, X, FAR)),
-    (1, 256, 256, (FAR, X, Y, NEXT)),
+    (0, 0, 256, (Y, X, NEXT, FAR)),
+    (0, 256, 256, (X, Y, ZED)),
+    (1, 0, 256, (NEXT, X, Y, FAR)),
+    (1, 256, 256, (FAR, NEXT, X, Y)),
 )
 CHUNKS = (
+    (CORE, Y, FAR, X, NEXT),
     (CORE, X, Y, ZED),
-    (CORE, X, Y, ZED),
-    (CORE, ZED, X, Y),
-    (CORE, Y, ZED, X),
+    (CORE, Y, X, ZED),
+    (CORE, ZED, Y, X),
     (CORE, Y, X, ZED),
     (WIDE, Y, ZED),
 )
@@ -896,115 +896,119 @@
         (n.f_near, 1),
     )
     plan[(At.W_OUTPUT,)] = (
+        (n.v_core,),
+        (n.f_step, 1, 0),
         (n.a_core, 0),
-        (n.f_step, 1, 0),
-        (n.v_core,),
         (n.f_step, 0, 0),
     )
-    plan[(At.VALUES, 6)] = (
+    plan[(At.VALUES, 5)] = (
+        (n.v_next, 0),
+    )
+    plan[(At.VALUES, 7)] = (
         (n.a_step, 0, 0),
-        (n.v_next, 0),
     )
     plan[(At.W_VALUE,)] = (
         (n.a_core, 1),
     )
     plan[(At.SCORES, 1)] = (
         (n.f_step, 0, 1),
+        (n.f_step, 1, 1),
     )
     plan[(At.SCORES, 2)] = (
         (n.a_core, 2),
         (n.a_step, 1, 0),
         (n.f_step, 2, 0),
+        (n.v_next, 1),
     )
     plan[(At.SCORES, 3)] = (
         (n.a_step, 0, 1),
     )
     plan[(At.SCORES, 4)] = (
+        (n.a_step, 2, 0),
         (n.a_core, 3),
-        (n.a_step, 2, 0),
-        (n.v_next, 1),
+        (n.f_step, 3, 0),
     )
     plan[(At.SCORES, 5)] = (
-        (n.f_step, 3, 0),
+        (n.f_step, 0, 2),
+        (n.v_next, 2),
     )
     plan[(At.SCORES, 6)] = (
-        (n.f_step, 1, 1),
         (n.a_step, 3, 0),
+        (n.a_step, 1, 1),
         (n.a_core, 4),
-        (n.a_step, 1, 1),
-        (n.f_step, 2, 1),
     )
     plan[(At.SCORES, 7)] = (
-        (n.a_step, 0, 2),
+        (n.f_step, 1, 2),
+        (n.a_step, 2, 1),
     )
     plan[(At.SCORES, 8)] = (
         (n.a_core, 5),
+        (n.a_step, 0, 2),
+        (n.f_step, 2, 1),
         (n.a_step, 4, 0),
-        (n.f_step, 0, 2),
-        (n.v_next, 2),
+        (n.f_step, 3, 1),
     )
     plan[(At.INPUT, 1)] = (
-        (n.a_step, 2, 1),
+        (n.f_step, 0, 3),
+        (n.v_next, 3),
+        (n.a_step, 1, 2),
+    )
+    plan[(At.INPUT, 3)] = (
+        (n.a_step, 2, 2),
+    )
+    plan[(At.END,)] = (
+        (n.f_step, 2, 2),
         (n.a_step, 3, 1),
-        (n.f_step, 3, 1),
-    )
-    plan[(At.INPUT, 3)] = (
-        (n.a_step, 1, 2),
-        (n.f_step, 1, 2),
-        (n.f_step, 2, 2),
-    )
-    plan[(At.END,)] = (
         (n.a_step, 4, 1),
         (n.a_step, 0, 3),
         (n.a_step, 5, 0),
-        (n.v_next, 3),
-        (n.a_step, 2, 2),
+        (n.f_back, 1, 0),
+        (n.f_back, 0, 0),
         (n.f_step, 3, 2),
-        (n.f_step, 1, 3),
-        (n.f_back, 0, 0),
+        (n.a_step, 3, 2),
+        (n.v_next, 4),
         (n.a_step, 4, 2),
-        (n.a_step, 3, 2),
+        (n.a_step, 0, 4),
         (n.a_step, 5, 1),
         (n.a_step, 1, 3),
+        (n.a_step, 3, 3),
+        (n.f_back, 0, 1),
         (n.a_step, 2, 3),
         (n.f_step, 2, 3),
+        (n.f_back, 1, 1),
+        (n.a_back, 0, 4),
         (n.f_step, 3, 3),
-        (n.f_back, 1, 0),
-        (n.a_step, 3, 3),
-        (n.a_back, 0, 3),
-        (n.v_next, 4),
-        (n.f_back, 0, 1),
-        (n.a_back, 2, 3),
+        (n.a_back, 3, 3),
         (n.a_step, 4, 3),
         (n.a_step, 5, 2),
-        (n.a_back, 3, 3),
+        (n.a_back, 0, 3),
+        (n.f_back, 0, 2),
+        (n.a_back, 1, 3),
         (n.f_back, 3, 0),
-        (n.a_back, 1, 3),
+        (n.a_back, 2, 3),
+        (n.a_back, 3, 2),
         (n.f_back, 2, 0),
-        (n.a_back, 0, 2),
-        (n.a_back, 2, 2),
-        (n.f_back, 1, 1),
-        (n.f_back, 3, 1),
         (n.a_back, 4, 3),
         (n.a_back, 5, 2),
+        (n.a_back, 2, 2),
         (n.a_back, 1, 2),
-        (n.a_back, 3, 2),
+        (n.f_back, 3, 1),
+        (n.a_back, 0, 2),
         (n.f_back, 2, 1),
-        (n.a_back, 0, 1),
         (n.a_back, 4, 2),
+        (n.a_back, 5, 1),
         (n.a_back, 2, 1),
-        (n.a_back, 5, 1),
-        (n.f_back, 1, 2),
-        (n.a_back, 0, 0),
         (n.a_back, 3, 1),
         (n.a_back, 1, 1),
         (n.a_back, 2, 0),
+        (n.a_back, 0, 1),
+        (n.a_back, 3, 0),
+        (n.a_back, 1, 0),
         (n.a_back, 4, 1),
+        (n.f_back, 2, 2),
+        (n.a_back, 0, 0),
+        (n.a_back, 5, 0),
         (n.f_back, 3, 2),
-        (n.a_back, 3, 0),
-        (n.f_back, 2, 2),
-        (n.a_back, 1, 0),
-        (n.a_back, 5, 0),
         (n.a_back, 4, 0),
     )
     plan[(At.BRANCH,)] = (

time: 111 us -> 109 us (0.982)
  Pallas kernels: 109 us -> 107 us
    pallas_call x1, Pallas kernels: 101 us -> 98.4 us  [tuned_layer(): pl.pallas_call(functools.partial(tuned_kernel, names), out_shape=list(out...]
where the time goes in v4:
time: 109 us; the launch traced here: 108 us
  Pallas kernels  107 us (98%)
  between operations  1.51 us (1%)
    pallas_call x1, Pallas kernels, tuned_layer(): pl.pallas_call(functools.partial(tuned_kernel, names), out_shape=list(out...  98.4 us
    pallas_call x1, Pallas kernels, widen(): pl.pallas_call(widen_kernel, out_shape=[o[0] for o in outs], in_specs=[AN...  8.53 us

profile of v4, /device:TPU:1, one launch (start us, length us, event | category | flops | bytes accessed | tf_op | source)
XLA Modules:
  0.0 108.4 jit_solution(6186681129761062353)
XLA Ops:
  1.3 98.4 %shard_map.280 = (bf16[1024,512]{1,0:T(8,128)(2,1)}, f32[1024,512]{1,0:T(8,128)}, f32[1024,512]{1,0:T(8,128)}, bf16[2,512,512]{2,1,0:T(8,128)(2,1)}, bf16[2,512,...) custom-call(bf16[1024,512]{1,0:T(8,128)(2,1)} %refs_0_.1, bf16[512,512]{1,0:T(8,128)(2,1)} %refs_1_.1, ...), custom_call_target="tpu_custom_call" | custom-call | flops 24999999488 | bytes 31457280 | tf_op jit(solution)/shard_map/pallas_call | solution.py:1091
  99.7 8.5 %shard_map.281 = (bf16[1024,512]{1,0:T(8,128)(2,1)}, f32[1024,512]{1,0:T(8,128)}, f32[1024,512]{1,0:T(8,128)}, f32[512,512]{1,0:T(8,128)}, f32[512,512]{1,0:T(8,...) custom-call(bf16[1024,512]{1,0:T(8,128)(2,1)} %get-tuple-element.37., ...), custom_call_target="tpu_custom_call" | custom-call | bytes 19922944 | tf_op jit(solution)/shard_map/pallas_call | solution.py:1156

commit v5 on v4

--- a/solution.py
+++ b/solution.py
@@ -18,18 +18,18 @@
 HALF_UNROLL = NORM_UNROLL = SECOND_UNROLL = FIRST_UNROLL = INPUT_UNROLL = 2
 CORE, X, Y, NEXT, FAR, ZED, WIDE, BATCH = range(8)
 UNITS = (
-    (0, 0, 256, (Y, X, NEXT, FAR)),
-    (0, 256, 256, (X, Y, ZED)),
-    (1, 0, 256, (NEXT, X, Y, FAR)),
-    (1, 256, 256, (FAR, NEXT, X, Y)),
+    (0, 0, 256, (X, Y, NEXT, FAR)),
+    (0, 256, 256, (Y, X, ZED)),
+    (1, 0, 256, (FAR, Y, NEXT, X)),
+    (1, 256, 256, (NEXT, X, Y, FAR)),
 )
 CHUNKS = (
-    (CORE, Y, FAR, X, NEXT),
+    (CORE, X, Y, NEXT, FAR),
+    (CORE, Y, X, FAR, NEXT),
+    (CORE, NEXT, Y, X, FAR),
+    (CORE, NEXT, X, FAR, Y),
+    (CORE, Y, X, ZED),
     (CORE, X, Y, ZED),
-    (CORE, Y, X, ZED),
-    (CORE, ZED, Y, X),
-    (CORE, Y, X, ZED),
-    (WIDE, Y, ZED),
 )
 
 bf16 = jnp.bfloat16
@@ -897,9 +897,9 @@
     )
     plan[(At.W_OUTPUT,)] = (
         (n.v_core,),
-        (n.f_step, 1, 0),
         (n.a_core, 0),
         (n.f_step, 0, 0),
+        (n.f_step, 1, 0),
     )
     plan[(At.VALUES, 5)] = (
         (n.v_next, 0),
@@ -915,101 +915,107 @@
         (n.f_step, 1, 1),
     )
     plan[(At.SCORES, 2)] = (
+        (n.a_step, 1, 0),
         (n.a_core, 2),
-        (n.a_step, 1, 0),
+        (n.v_next, 1),
+    )
+    plan[(At.SCORES, 4)] = (
+        (n.a_core, 3),
+        (n.a_step, 0, 1),
+        (n.f_step, 3, 0),
+        (n.a_step, 2, 0),
         (n.f_step, 2, 0),
-        (n.v_next, 1),
-    )
-    plan[(At.SCORES, 3)] = (
-        (n.a_step, 0, 1),
-    )
-    plan[(At.SCORES, 4)] = (
-        (n.a_step, 2, 0),
-        (n.a_core, 3),
-        (n.f_step, 3, 0),
     )
     plan[(At.SCORES, 5)] = (
         (n.f_step, 0, 2),
-        (n.v_next, 2),
     )
     plan[(At.SCORES, 6)] = (
+        (n.a_core, 4),
         (n.a_step, 3, 0),
         (n.a_step, 1, 1),
-        (n.a_core, 4),
     )
     plan[(At.SCORES, 7)] = (
         (n.f_step, 1, 2),
+        (n.v_next, 2),
         (n.a_step, 2, 1),
+        (n.a_step, 0, 2),
     )
     plan[(At.SCORES, 8)] = (
         (n.a_core, 5),
-        (n.a_step, 0, 2),
-        (n.f_step, 2, 1),
         (n.a_step, 4, 0),
         (n.f_step, 3, 1),
     )
     plan[(At.INPUT, 1)] = (
+        (n.a_step, 1, 2),
+        (n.f_step, 2, 1),
+        (n.a_step, 3, 1),
         (n.f_step, 0, 3),
+    )
+    plan[(At.INPUT, 3)] = (
+        (n.a_step, 5, 0),
+        (n.a_step, 2, 2),
+    )
+    plan[(At.END,)] = (
         (n.v_next, 3),
-        (n.a_step, 1, 2),
-    )
-    plan[(At.INPUT, 3)] = (
-        (n.a_step, 2, 2),
-    )
-    plan[(At.END,)] = (
-        (n.f_step, 2, 2),
-        (n.a_step, 3, 1),
         (n.a_step, 4, 1),
         (n.a_step, 0, 3),
-        (n.a_step, 5, 0),
         (n.f_back, 1, 0),
+        (n.a_step, 3, 2),
+        (n.f_step, 3, 2),
+        (n.f_step, 2, 2),
+        (n.a_step, 1, 3),
+        (n.a_step, 5, 1),
         (n.f_back, 0, 0),
-        (n.f_step, 3, 2),
-        (n.a_step, 3, 2),
+        (n.a_step, 2, 3),
+        (n.a_step, 4, 2),
         (n.v_next, 4),
-        (n.a_step, 4, 2),
+        (n.a_step, 1, 4),
+        (n.f_step, 2, 3),
         (n.a_step, 0, 4),
-        (n.a_step, 5, 1),
-        (n.a_step, 1, 3),
         (n.a_step, 3, 3),
+        (n.f_back, 1, 1),
+        (n.a_step, 5, 2),
         (n.f_back, 0, 1),
-        (n.a_step, 2, 3),
-        (n.f_step, 2, 3),
-        (n.f_back, 1, 1),
+        (n.f_step, 3, 3),
+        (n.a_step, 2, 4),
+        (n.a_back, 1, 4),
+        (n.a_step, 3, 4),
+        (n.f_back, 2, 0),
+        (n.a_step, 4, 3),
         (n.a_back, 0, 4),
-        (n.f_step, 3, 3),
+        (n.a_step, 5, 3),
+        (n.f_back, 3, 0),
+        (n.a_back, 2, 4),
+        (n.f_back, 0, 2),
+        (n.a_back, 3, 4),
+        (n.a_back, 0, 3),
+        (n.a_back, 1, 3),
+        (n.f_back, 2, 1),
+        (n.a_back, 2, 3),
+        (n.a_back, 4, 3),
+        (n.f_back, 3, 1),
         (n.a_back, 3, 3),
-        (n.a_step, 4, 3),
-        (n.a_step, 5, 2),
-        (n.a_back, 0, 3),
-        (n.f_back, 0, 2),
-        (n.a_back, 1, 3),
-        (n.f_back, 3, 0),
-        (n.a_back, 2, 3),
+        (n.a_back, 5, 3),
+        (n.a_back, 0, 2),
+        (n.a_back, 1, 2),
+        (n.a_back, 2, 2),
+        (n.a_back, 4, 2),
         (n.a_back, 3, 2),
-        (n.f_back, 2, 0),
-        (n.a_back, 4, 3),
         (n.a_back, 5, 2),
-        (n.a_back, 2, 2),
-        (n.a_back, 1, 2),
-        (n.f_back, 3, 1),
-        (n.a_back, 0, 2),
-        (n.f_back, 2, 1),
-        (n.a_back, 4, 2),
+        (n.f_back, 3, 2),
+        (n.a_back, 0, 1),
+        (n.f_back, 2, 2),
+        (n.a_back, 1, 1),
+        (n.a_back, 2, 1),
         (n.a_back, 5, 1),
-        (n.a_back, 2, 1),
+        (n.a_back, 4, 1),
         (n.a_back, 3, 1),
-        (n.a_back, 1, 1),
+        (n.a_back, 0, 0),
+        (n.a_back, 1, 0),
         (n.a_back, 2, 0),
-        (n.a_back, 0, 1),
+        (n.a_back, 5, 0),
+        (n.a_back, 4, 0),
         (n.a_back, 3, 0),
-        (n.a_back, 1, 0),
-        (n.a_back, 4, 1),
-        (n.f_back, 2, 2),
-        (n.a_back, 0, 0),
-        (n.a_back, 5, 0),
-        (n.f_back, 3, 2),
-        (n.a_back, 4, 0),
     )
     plan[(At.BRANCH,)] = (
         (n.arrived_near, 1),

time: 109 us -> 107 us (0.982)
  Pallas kernels: 107 us -> 105 us
    pallas_call x1, Pallas kernels: 98.4 us -> 96.4 us  [tuned_layer(): pl.pallas_call(functools.partial(tuned_kernel, names), out_shape=list(out...]
where the time goes in v5:
time: 107 us; the launch traced here: 106 us
  Pallas kernels  105 us (98%)
  between operations  1.51 us (1%)
    pallas_call x1, Pallas kernels, tuned_layer(): pl.pallas_call(functools.partial(tuned_kernel, names), out_shape=list(out...  96.4 us
    pallas_call x1, Pallas kernels, widen(): pl.pallas_call(widen_kernel, out_shape=[o[0] for o in outs], in_specs=[AN...  8.53 us

profile of v5, /device:TPU:1, one launch (start us, length us, event | category | flops | bytes accessed | tf_op | source)
XLA Modules:
  0.0 106.5 jit_solution(3512830680805750417)
XLA Ops:
  1.3 96.4 %shard_map.280 = (bf16[1024,512]{1,0:T(8,128)(2,1)}, f32[1024,512]{1,0:T(8,128)}, f32[1024,512]{1,0:T(8,128)}, bf16[2,512,512]{2,1,0:T(8,128)(2,1)}, bf16[2,512,...) custom-call(bf16[1024,512]{1,0:T(8,128)(2,1)} %refs_0_.1, bf16[512,512]{1,0:T(8,128)(2,1)} %refs_1_.1, ...), custom_call_target="tpu_custom_call" | custom-call | flops 24999999488 | bytes 31457280 | tf_op jit(solution)/shard_map/pallas_call | solution.py:1097
  97.7 8.5 %shard_map.281 = (bf16[1024,512]{1,0:T(8,128)(2,1)}, f32[1024,512]{1,0:T(8,128)}, f32[1024,512]{1,0:T(8,128)}, f32[512,512]{1,0:T(8,128)}, f32[512,512]{1,0:T(8,...) custom-call(bf16[1024,512]{1,0:T(8,128)(2,1)} %get-tuple-element.37., ...), custom_call_target="tpu_custom_call" | custom-call | bytes 19922944 | tf_op jit(solution)/shard_map/pallas_call | solution.py:1162
